TPU v7x, 256 devices: a whole 4x4x8 slice. The times are simulated.
256 devices in a mesh: date: 8 (over x, core), space: 32 (over z, y).
Axes of the slice: x: 4, y: 4, z: 8, core: 2. Of those that a mesh axis runs over, the one named last changes fastest.
Arguments:
- backscatter: float32 [64, 2, 512, 2048], P('date', None, 'space'), may hold values from 0.01 to 1
- edge_dirs: int32 [64, 512, 2048], P('date', 'space'), may hold values from 0 to 7
- labels: int32 [512, 2048], P('space', 'date'), may hold values from 0 to 4095, as said below
- parcel_slot: int32 [4096], replicated, may hold values from 0 to 4095, as said below
Outputs:
- series_coeffs: bfloat16 [512, 2048, 128], P('space', 'date')
- parcel_means: float32 [4096, 128], P(('date', 'space'))
Inputs may be any that keep to these rules, and one draw needn't show every extreme that they name: `labels`: each parcel's pixels form four fields, in two neighbouring row strips of 16 rows (the first starting at an even multiple of 16) and two column ranges 2048 / 2 columns apart, each range lying within one block of 256 columns (the columns of one `date` index); parcels that no pixel names may exist. `parcel_slot`: a permutation of the parcels that puts each parcel's output row on one of the four devices holding its fields (device index = date index * 32 + space index, 16 rows each).
All inputs are finite; a program needn't handle non-finite values.
Results may differ from a plain program's by a relative error of at most 0.0049.
Values may be sent and summed in bfloat16 or wider, within the bound.
A program may use at most 64 MiB of HBM per device.

v0:
```python
import jax
import jax.numpy as jnp
from jax import lax
from jax.sharding import PartitionSpec as P

DATES = 64


vectors = ((1, 0), (1, 1), (0, 1), (-1, 1), (-1, 0), (-1, -1), (0, -1), (1, -1))
speckle = 0.25


def padded_2(value, sides, width):
    for axis, dim in sides:
        count, length = (lax.axis_size(axis), value.shape[dim])
        up = [(i, (i + 1) % count) for i in range(count - 1)]
        down = [(j, i) for i, j in up]
        last = lax.slice_in_dim(value, length - width, length, axis=dim)
        first = lax.slice_in_dim(value, 0, width, axis=dim)
        before = lax.ppermute(last, axis, up)
        after = lax.ppermute(first, axis, down)
        value = jnp.concatenate([before, value, after], axis=dim)
    return value


def lee_filter(padded, masks, nrows, ncols):
    first = [None] * 8
    second = [None] * 8
    for i in range(-3, 4):
        for j in range(-3, 4):
            piece = padded[..., 3 + i : 3 + i + nrows, 3 + j : 3 + j + ncols]
            square = piece * piece
            for d in range(8):
                if i * vectors[d][0] + j * vectors[d][1] >= 0:
                    first[d] = piece if first[d] is None else first[d] + piece
                    second[d] = square if second[d] is None else second[d] + square
    centre = padded[..., 3 : 3 + nrows, 3 : 3 + ncols]
    sel_first = jnp.zeros_like(centre)
    sel_second = jnp.zeros_like(centre)
    for d in range(8):
        hit = masks == d
        sel_first = jnp.where(hit, first[d], sel_first)
        sel_second = jnp.where(hit, second[d], sel_second)
    mean = sel_first / 28.0
    var = sel_second / 28.0 - mean * mean
    noise = speckle * mean * mean
    signal = jnp.maximum((var - noise) / (1.0 + speckle), 0.0)
    gainv = signal / (signal + noise)
    filtered = mean + gainv * (centre - mean)
    return jnp.log10(filtered).astype(jnp.bfloat16)


def make_basis(count):
    times = jnp.arange(count, dtype=jnp.float32)[:, None]
    index = jnp.arange(count, dtype=jnp.float32)[None, :]
    half = count // 2
    cosine = jnp.cos(2.0 * jnp.pi * index * times / count)
    sine = jnp.sin(2.0 * jnp.pi * (index - half) * times / count)
    table = jnp.where(index <= half, cosine, sine) * jnp.sqrt(2.0 / count)
    return table.astype(jnp.bfloat16)


def local(backscatter, edge_dirs, labels, parcel_slot):
    date_local, pols, nrows, ncols = backscatter.shape
    tall = padded_2(backscatter, (("space", 2),), 3)
    padded = jnp.pad(tall, ((0, 0), (0, 0), (0, 0), (3, 3)))
    level = lee_filter(padded, edge_dirs[:, None], nrows, ncols)
    basis = make_basis(DATES)
    col_local = labels.shape[1]
    series = lax.all_to_all(level, "date", split_axis=3, concat_axis=0, tiled=True)
    part_rows = series.shape[2]
    coeffs = jnp.einsum("tprc,tj->rcpj", series, basis, preferred_element_type=jnp.float32)
    coeffs = coeffs.reshape(part_rows, col_local, pols * DATES)
    series_coeffs = coeffs.astype(jnp.bfloat16)
    feats = series_coeffs.shape[2]
    parcels = parcel_slot.shape[0]
    pixels = nrows * col_local
    block = min(512, pixels)
    slots = jnp.take(parcel_slot, labels.reshape(-1))
    flat = series_coeffs.reshape(pixels // block, block, feats)
    slot_blocks = slots.reshape(pixels // block, block)
    targets = jnp.arange(parcels, dtype=jnp.int32)[:, None]

    def accumulate(carry, inputs):
        sums, counts = carry
        values, slot_row = inputs
        onehot = (targets == slot_row[None, :]).astype(jnp.bfloat16)
        sums = sums + jnp.dot(onehot, values, preferred_element_type=jnp.float32)
        counts = counts + jnp.sum(onehot, axis=1, dtype=jnp.float32)
        return ((sums, counts), None)

    start_carry = (jnp.zeros((parcels, feats), jnp.float32), jnp.zeros((parcels,), jnp.float32))
    (sums, counts), unused = lax.scan(accumulate, start_carry, (flat, slot_blocks))
    owned_sums, owned_counts = (
        lax.psum_scatter(sums, ("date", "space"), scatter_dimension=0, tiled=True),
        lax.psum_scatter(counts, ("date", "space"), scatter_dimension=0, tiled=True),
    )
    parcel_means = owned_sums / jnp.maximum(owned_counts, 1.0)[:, None]
    return (series_coeffs, parcel_means)


def solution(mesh):
    placed = (P("date", None, "space", None), P("date", "space", None), P("space", "date"), P())
    return jax.shard_map(
        local,
        mesh=mesh,
        in_specs=placed,
        out_specs=(P("space", "date", None), P(("date", "space"), None)),
        check_vma=False,
    )
```

profile of v0, /device:TPU:0, one launch (start us, length us, event | category | flops | bytes accessed | tf_op | source)
XLA Modules:
  0.0 1466.7 jit_solution(17883722546654773009)
XLA Ops:
  7.2 0.0 copy-start
  7.2 0.0 copy-start.2
  7.2 1.8 fusion.115
  9.0 0.2 copy.130
  9.3 0.0 copy-start.3
  9.3 0.0 copy-start.1
  9.3 1.4 collective-permute-start.1
  10.7 0.2 copy.129
  11.0 4.6 collective-permute-start
  15.6 0.0 copy-done.2
  15.6 1.4 broadcast_compare_fusion.7
  17.0 0.0 copy-done.3
  17.0 0.0 copy-done.1
  17.0 0.2 constant_dynamic-update-slice_fusion.1
  17.3 4.5 collective-permute-done
  21.7 0.3 copy.116
  22.0 0.0 collective-permute-done.1
  22.0 0.4 constant_dynamic-update-slice_fusion
  22.4 1.6 select_maximum_fusion
  24.1 42.1 %fusion.96 = bf16[8,2,16,2048]{3,2,1,0:T(8,128)(2,1)S(1)} fusion(f32[8,2,16,2048]{3,2,1,0:T(8,128)S(1)} %copy-done.1, f32[8,2,22,2054]{3,2,1,0:T(8,128)S(1)} %select_maximum_fusion, f32[8,2,3,2048]{3,2,1,0:T(4,128)S(1)} %copy.116, f32[8,2,19,2048]{3,2,1,0:T(8,128)S(1)} %get-tuple-element.112, pred[8,16,2048]{2,1,0:T(8,128)(4,1)S(1)} %get-tuple-element.110, ...), kind=kLoop, calls=%fused_computation.116 | loop fusion | flops 248512512 | bytes 100007936 | tf_op jit(solution)/shard_map/convert_element_type | solution.py:50
  66.2 8.5 copy.120
  74.7 11.2 reshape.97
  86.0 4.5 all-to-all-start
  90.4 0.2 reduce-scatter.2.cloned.1.call-start
  90.7 0.0 copy-done
  90.7 23.0 %gather_fusion = s32[4096]{0:T(1024)S(1)} fusion(s32[4096]{0:T(1024)S(1)} %copy-done, s32[4096]{0:T(1024)S(1)} %broadcast_clamp_fusion), kind=kCustom, calls=%fused_computation | custom fusion | bytes 49152 | tf_op jit(solution)/shard_map/jit(_take)/gather | solution.py:79
  113.8 0.0 all-to-all-done
  113.9 7.6 reshape.98
  121.4 8.9 copy.121
  130.3 0.7 fusion.97
  131.0 1.5 copy.127
  132.5 1.8 reshape.96
  134.3 43.5 %while.13 = (s32[]{:T(128)}, f32[4096,128]{1,0:T(8,128)}, f32[4096]{0:T(1024)S(1)}, s32[8,512]{1,0:T(8,128)S(1)}, bf16[8,512,128]{2,1,0:T(8,128)(2,1)}, /*index=5*/s32[]{:T(128)}, s32[]{:T(128)}) while((s32[]{:T(128)}, f32[4096,128]{1,0:T(8,128)}, f32[4096]{0:T(1024)S(1)}, s32[8,512]{1,0:T(8,128)S(1)}, ...), condition=%wide.region_2.3_spmd.clone, body=%wide.region_0.2_spmd.clone.sunk | while | flops 548409344 | bytes 4399708 | solution.py:93
  134.3 3.8 fusion.119
  138.0 1.0 convert_reduce_fusion.2
  139.0 4.5 fusion.119
  143.6 1.0 convert_reduce_fusion.2
  144.6 4.5 fusion.119
  149.1 1.0 convert_reduce_fusion.2
  150.1 4.5 fusion.119
  154.7 1.0 convert_reduce_fusion.2
  155.7 4.5 fusion.119
  160.2 1.0 convert_reduce_fusion.2
  161.2 4.5 fusion.119
  165.7 1.0 convert_reduce_fusion.2
  166.8 4.5 fusion.119
  171.3 1.0 convert_reduce_fusion.2
  172.3 4.5 fusion.119
  176.8 1.0 convert_reduce_fusion.2
  177.8 0.0 reduce-scatter.2.cloned.1.call-update
  177.8 0.1 copy.122
  177.9 1.3 copy.125
  179.3 86.1 %all-reduce.1 = f32[4096]{0:T(1024)S(1)} all-reduce(f32[4096]{0:T(1024)S(1)} %get-tuple-element.36), channel_id=3, replica_groups=mesh['date'=8,'space'=32] {'date','space'}, use_global_device_ids=true, to_apply=%region_4.5.clone | all-reduce | flops 4096 | bytes 32768
  265.3 0.1 dynamic-slice_maximum_fusion
  265.4 1193.0 %reduce-scatter.2.cloned.1.call-done = f32[16,128]{1,0:T(8,128)} async-done(((f32[4096,128]{1,0:T(8,128)}), f32[16,128]{1,0:T(8,128)}) %reduce-scatter.2.cloned.1.call-update) | async-done | bytes 8208 | tf_op jit(solution)/shard_map/reduce_scatter | solution.py:95
  1458.4 1.4 broadcast_divide_fusion
  (26 shorter events, 0.2 us)
Async XLA Ops:
  7.2 83.6 %copy-start = (s32[4096]{0:T(1024)S(1)}, s32[4096]{0:T(1024)}, u32[]{:S(2)}) copy-start(s32[4096]{0:T(1024)} %param.9) | copy-start | bytes 49156
  7.2 8.4 copy-start.2
  9.3 7.7 copy-start.3
  9.3 7.7 copy-start.1
  9.3 12.7 collective-permute-start.1
  11.0 10.7 collective-permute-start
  86.0 27.9 %all-to-all-start = ((bf16[8,2,32768]{2,1,0:T(2,128)(2,1)}), bf16[8,2,32768]{2,1,0:T(2,128)(2,1)S(1)}, u32[]{:S(2)}, u32[]{:S(2)}) async-start(bf16[8,2,32768]{2,1,0:T(2,128)(2,1)} %reshape.97), calls=%async_computation | async-start | bytes 2097152 | tf_op jit(solution)/shard_map/all_to_all | solution.py:70
  90.4 1368.0 %reduce-scatter.2.cloned.1.call-start = ((), (), s32[]{:S(2)}) async-start(), calls=%async_computation.2 | async-start | bytes 2105344 | tf_op jit(solution)/shard_map/reduce_scatter | solution.py:95
Sparse Core Ops, SparseCore 0:
  178.0 1280.4 reduce-scatter.1
where the time goes:
time: 1470 us
  waiting for transfers between devices  1200 us (82%)
  blocking collectives  86.1 us (6%)
  local copies, waits for them, and re-layouts  67.3 us (5%)
  other arithmetic  54.4 us (4%)
  matrix products  36.1 us (2%)
    reduce_scatter x1, waiting for transfers between devices, local(): lax.psum_scatter(sums, ('date', 'space'), scatter_dimension=0, tiled=True)  1190 us
    unnamed x1, blocking collectives  86.1 us
    convert_element_type x1, other arithmetic, lee_filter(): return jnp.log10(filtered).astype(jnp.bfloat16)  42.1 us
    dot_general x8, matrix products, accumulate(): sums = sums + jnp.dot(onehot, values, preferred_element_type=jnp.float32)  35.4 us
  transfers between devices with their start and end apart: 4, of which 2 were waited for; matrix products, arithmetic and copies ran while one was open for 2% of the time, Pallas kernels for 0%

commit v1 on v0

v1 whole, which is shorter than its diff:
```python
import functools

import jax
import jax.numpy as jnp
import ml_dtypes
import numpy as np
from jax import lax
from jax.experimental import pallas as pl
from jax.experimental.pallas import tpu as pltpu
from jax.sharding import PartitionSpec as P

MESH = pl.DeviceIdType.MESH
F32 = jnp.float32
BF16 = jnp.bfloat16
DATES = 64
ROWS = 16
TALL = ROWS + 6
ZERO = TALL
LOG10E = 0.4342944819032518


def basis_table(dates, group, pols):
    times = np.arange(dates, dtype=np.float32)[:, None]
    index = np.arange(dates, dtype=np.float32)[None, :]
    half = dates // 2
    scale = np.sqrt(np.float32(2.0 / dates))
    cosine = np.cos(np.float32(2.0 * np.pi) * index * times / np.float32(dates))
    sine = np.sin(np.float32(2.0 * np.pi) * (index - half) * times / np.float32(dates))
    table = (np.where(index <= half, cosine, sine) * scale).astype(np.float32)
    wide = np.zeros((dates // group, pols, group, pols, dates), np.float32)
    for p in range(pols):
        wide[:, p, :, p, :] = table.reshape(dates // group, group, dates)
    return wide.reshape(dates * pols, pols * dates).astype(ml_dtypes.bfloat16)


def kernel(
    ndate, nspace, wide,
    x_hbm, e_hbm, labels_ref, slot_ref, basis_ref,
    out_ref, means_ref,
    xin, ein, a0, r7, xp, xm, d1, d2, vv, vm, tt, p2, hh, sendbuf, got, onehot, acc, qgot,
    in_sem, halo_send, halo_recv, send_sem, recv_sem, own_sem, qsend, qrecv,
):
    full = wide + 128
    date = lax.axis_index("date")
    space = lax.axis_index("space")
    half = ndate // 2

    order = list(range(3)) + list(range(ROWS - 3, ROWS)) + list(range(3, ROWS - 3))

    def loads(r):
        for p in range(2):
            yield pltpu.make_async_copy(x_hbm.at[:, p, r, :], xin.at[r + 3, p, :, 0:wide], in_sem.at[r, p])
        yield pltpu.make_async_copy(e_hbm.at[:, r, :], ein.at[r], in_sem.at[r, 2])

    for r in order:
        for copy in loads(r):
            copy.start()

    barrier = pltpu.get_barrier_semaphore()
    for k in range(1, ndate):
        pl.semaphore_signal(barrier, inc=1, device_id={"date": lax.rem(date + k, ndate)}, device_id_type=MESH)
    mate = space + 1 - 2 * lax.rem(space, 2)
    opposite = lax.rem(date + half, ndate)
    pl.semaphore_signal(barrier, inc=1, device_id={"date": opposite, "space": mate}, device_id_type=MESH)

    @pl.when(space > 0)
    def _():
        pl.semaphore_signal(barrier, inc=1, device_id={"space": space - 1}, device_id_type=MESH)

    @pl.when(space < nspace - 1)
    def _():
        pl.semaphore_signal(barrier, inc=1, device_id={"space": space + 1}, device_id_type=MESH)

    xin[:, :, :, wide:] = jnp.zeros((TALL, 2, 8, 128), F32)
    zero_row = jnp.zeros((2, 8, full), F32)
    for q in range(2):
        a0[q, ZERO] = zero_row
        r7[q, ZERO] = zero_row[:, :, :wide]
        p2[q, ZERO] = zero_row[:, :, :wide]
    xp[ZERO] = zero_row
    xm[ZERO] = zero_row

    base_date = lax.rem(date, half)
    base_space = space - lax.rem(space, 2)
    parts = []
    for u in range(4):
        owner = (base_date + (u // 2) * half) * nspace + base_space + u % 2
        parts.append(lax.broadcasted_iota(jnp.int32, (ROWS, 128), 0) + owner * ROWS)
    ids = jnp.concatenate(parts, axis=0)
    lane = lax.broadcasted_iota(jnp.int32, (4 * ROWS, 128), 1).astype(F32)
    total = jnp.zeros((4 * ROWS, 128), F32)
    for g in range(slot_ref.shape[0]):
        total = total + jnp.where(ids == slot_ref[g : g + 1, :], lane + float(128 * g), 0.0)
    parcel_of = jnp.sum(total, axis=1, keepdims=True).astype(jnp.int32)
    for r in range(ROWS):
        onehot[r] = jnp.where(parcel_of == labels_ref[r : r + 1, :], 1.0, 0.0).astype(BF16)

    def down():
        return pltpu.make_async_remote_copy(
            src_ref=xin.at[ROWS : ROWS + 3, :, :, 0:wide], dst_ref=xin.at[0:3, :, :, 0:wide],
            send_sem=halo_send.at[0], recv_sem=halo_recv.at[0],
            device_id={"space": space + 1}, device_id_type=MESH)

    def up():
        return pltpu.make_async_remote_copy(
            src_ref=xin.at[3:6, :, :, 0:wide], dst_ref=xin.at[ROWS + 3 : ROWS + 6, :, :, 0:wide],
            send_sem=halo_send.at[1], recv_sem=halo_recv.at[1],
            device_id={"space": space - 1}, device_id_type=MESH)

    degree = (ndate - 1) + 1 + jnp.where(space > 0, 1, 0) + jnp.where(space < nspace - 1, 1, 0)
    pl.semaphore_wait(barrier, degree)
    for r in list(range(3)) + list(range(ROWS - 3, ROWS)):
        for copy in loads(r):
            copy.wait()

    @pl.when(space < nspace - 1)
    def _():
        down().start()

    @pl.when(space > 0)
    def _():
        up().start()

    @pl.when(space == 0)
    def _():
        xin[0:3, :, :, 0:wide] = jnp.zeros((3, 2, 8, wide), F32)

    @pl.when(space == nspace - 1)
    def _():
        xin[ROWS + 3 : ROWS + 6, :, :, 0:wide] = jnp.zeros((3, 2, 8, wide), F32)

    def send(r):
        for k in range(1, ndate):
            peer = lax.rem(date + k, ndate)
            pltpu.make_async_remote_copy(
                src_ref=sendbuf.at[r, peer], dst_ref=got.at[r, date],
                send_sem=send_sem, recv_sem=recv_sem.at[r],
                device_id={"date": peer}, device_id_type=MESH).start()
        pltpu.make_async_copy(sendbuf.at[r, date], got.at[r, date], own_sem.at[r]).start()

    def left(v, n):
        return pltpu.roll(v, full - n, axis=1)

    def right(v, n):
        return pltpu.roll(v, n, axis=1)

    def back(i, s, n):
        return jnp.where(i - n >= s, i - n, ZERO)

    def phase1(i, s, fresh, emit):
        lo = back(i, s, 7)
        new = lax.rem(i, 2)
        old = 1 - new
        for p in range(2):
            if fresh:
                x = xin[i, p]
                for q in range(2):
                    v = x * x if q else x
                    pair = v + left(v, 1)
                    four = pair + left(pair, 2)
                    a0[q, i, p] = four
                    r7[q, i, p] = (four + right(four, 3) - v)[:, :wide]
                xp[i, p] = left(x, 3)
                xm[i, p] = right(x, 3)
            for q in range(2):
                def sq(v):
                    return v * v if q else v

                d1[new, q, p] = left(d1[old, q, p] - sq(xp[lo, p]), 1) + sq(xm[i, p])
                d2[new, q, p] = right(d2[old, q, p] - sq(xm[lo, p]), 1) + sq(xp[i, p])
                v = vv[q, p] + (a0[q, i, p] - a0[q, lo, p])
                vv[q, p] = v
                if emit:
                    vm[q, p] = right(v, 3)[:, :wide]

    def phase2(i, s, emit):
        lo = back(i, s, 7)
        new = lax.rem(i, 2)
        old = 1 - new
        r = i - 6
        for c in range(ndate):
            width = wide // ndate
            cols = slice(c * width, (c + 1) * width)
            if emit:
                e = ein[r, :, cols]
                b0 = ((e & 1) > 0)[None]
                b1 = ((e & 2) > 0)[None]
                b2 = ((e & 4) > 0)[None]
            sums = []
            for q in range(2):
                rn = r7[q, i, :, :, cols]
                ro = r7[q, lo, :, :, cols]
                d1n, d1o = d1[new, q, :, :, cols], d1[old, q, :, :, cols]
                d2n, d2o = d2[new, q, :, :, cols], d2[old, q, :, :, cols]
                t1 = tt[q, 0, :, :, cols] - d1o + rn
                t3 = tt[q, 1, :, :, cols] + d2n - ro
                t5 = tt[q, 2, :, :, cols] + d1n - ro
                t7 = tt[q, 3, :, :, cols] - d2o + rn
                pr = rn + r7[q, back(i, s, 1), :, :, cols]
                h = pr + p2[q, back(i, s, 2), :, :, cols]
                tt[q, 0, :, :, cols] = t1
                tt[q, 1, :, :, cols] = t3
                tt[q, 2, :, :, cols] = t5
                tt[q, 3, :, :, cols] = t7
                p2[q, i, :, :, cols] = pr
                hh[q, i, :, :, cols] = h
                if emit:
                    s02 = jnp.where(b1, vv[q, :, :, cols], h)
                    s46 = jnp.where(b1, vm[q, :, :, cols], hh[q, i - 3, :, :, cols])
                    s13 = jnp.where(b1, t3, t1)
                    s57 = jnp.where(b1, t7, t5)
                    sums.append(jnp.where(b2, jnp.where(b0, s57, s46), jnp.where(b0, s13, s02)))
            if emit:
                first, second = sums
                x = xin[i - 3, :, :, cols]
                mean = first * (1.0 / 28.0)
                sq_mean = mean * mean
                excess = jnp.maximum(second * (1.0 / 28.0) - 1.25 * sq_mean, 0.0)
                under = excess + 0.3125 * sq_mean
                inv = pl.reciprocal(under, approx=True)
                inv = inv * (2.0 - under * inv)
                filtered = mean + excess * inv * (x - mean)
                level = jnp.log(filtered) * LOG10E
                sendbuf[r, c] = level.reshape(2 * 8, width).astype(BF16)

    def reset():
        d1[...] = jnp.zeros(d1.shape, F32)
        d2[...] = jnp.zeros(d2.shape, F32)
        vv[...] = jnp.zeros(vv.shape, F32)
        tt[...] = jnp.zeros(tt.shape, F32)

    def step(s, fresh, emit):
        def body(i, carry):
            if fresh and s == 3:
                @pl.when(jnp.logical_and(i >= 6, i < ROWS))
                def _():
                    for copy in loads(i - 3):
                        copy.wait()
            phase1(i, s, fresh, emit)
            phase2(i, s, emit)
            if emit:
                send(i - 6)
            return carry

        return body

    reset()
    lax.fori_loop(3, 9, step(3, True, False), 0)
    lax.fori_loop(9, ROWS + 3, step(3, True, True), 0)

    @pl.when(space < nspace - 1)
    def _():
        up().wait_recv()

    lax.fori_loop(ROWS + 3, ROWS + 6, step(3, True, True), 0)

    @pl.when(space > 0)
    def _():
        down().wait_recv()

    reset()
    lax.fori_loop(0, 3, step(0, True, False), 0)
    lax.fori_loop(3, 6, step(0, False, False), 0)
    lax.fori_loop(6, 9, step(0, False, True), 0)

    acc[...] = jnp.zeros(acc.shape, F32)
    ones = jnp.ones((wide // ndate, 128), BF16)

    def fit(r):
        pltpu.make_async_copy(got.at[r, 0 : ndate - 1], got.at[r, 0 : ndate - 1], recv_sem.at[r]).wait()
        pltpu.make_async_copy(sendbuf.at[r, date], got.at[r, date], own_sem.at[r]).wait()
        series = got[r].reshape(ndate * 16, wide // ndate)
        coeffs = lax.dot_general(series, basis_ref[...], (((0,), (0,)), ((), ())), preferred_element_type=F32)
        coeffs = coeffs.astype(BF16)
        out_ref[r] = coeffs
        acc[...] += jnp.dot(onehot[r], jnp.concatenate([coeffs, ones], axis=1), preferred_element_type=F32)

    def fit_step(n, carry):
        fit(lax.rem(n + 3, ROWS))
        return carry

    lax.fori_loop(0, ROWS, fit_step, 0)

    high = date // half
    low = lax.rem(space, 2)
    copies = []
    for k in range(1, 4):
        far, near = k // 2, k % 2
        part = lax.rem(high + far, 2) * 2 + lax.rem(low + near, 2)
        copy = pltpu.make_async_remote_copy(
            src_ref=acc.at[pl.ds(pl.multiple_of(part * ROWS, ROWS), ROWS)], dst_ref=qgot.at[k - 1],
            send_sem=qsend.at[k - 1], recv_sem=qrecv.at[k - 1],
            device_id={"date": opposite if far else date, "space": mate if near else space}, device_id_type=MESH)
        copy.start()
        copies.append(copy)
    total = acc[pl.ds(pl.multiple_of((high * 2 + low) * ROWS, ROWS), ROWS), :]
    for k, copy in enumerate(copies):
        copy.wait_recv()
        total = total + qgot[k]
    means_ref[...] = total[:, :128] / jnp.maximum(total[:, 128:], 1.0)

    for copy in copies:
        copy.wait_send()
    pltpu.make_async_copy(sendbuf.at[:, 0 : ndate - 1], sendbuf.at[:, 0 : ndate - 1], send_sem).wait()

    @pl.when(space < nspace - 1)
    def _():
        down().wait_send()

    @pl.when(space > 0)
    def _():
        up().wait_send()


def solution(mesh):
    ndate, nspace = mesh.shape["date"], mesh.shape["space"]
    basis = basis_table(DATES, DATES // ndate, 2)

    def local(backscatter, edge_dirs, labels, parcel_slot):
        wide = backscatter.shape[3]
        full = wide + 128
        cols = wide // ndate
        any_spec = pl.BlockSpec(memory_space=pl.ANY)
        vmem = pl.BlockSpec(memory_space=pltpu.VMEM)
        return pl.pallas_call(
            functools.partial(kernel, ndate, nspace, wide),
            out_shape=(
                jax.ShapeDtypeStruct((ROWS, cols, 128), BF16),
                jax.ShapeDtypeStruct((ROWS, 128), F32),
            ),
            in_specs=[any_spec, any_spec, vmem, vmem, vmem],
            out_specs=(vmem, vmem),
            scratch_shapes=[
                pltpu.VMEM((TALL, 2, 8, full), F32),
                pltpu.VMEM((ROWS, 8, wide), jnp.int32),
                pltpu.VMEM((2, TALL + 1, 2, 8, full), F32),
                pltpu.VMEM((2, TALL + 1, 2, 8, wide), F32),
                pltpu.VMEM((TALL + 1, 2, 8, full), F32),
                pltpu.VMEM((TALL + 1, 2, 8, full), F32),
                pltpu.VMEM((2, 2, 2, 8, full), F32),
                pltpu.VMEM((2, 2, 2, 8, full), F32),
                pltpu.VMEM((2, 2, 8, full), F32),
                pltpu.VMEM((2, 2, 8, wide), F32),
                pltpu.VMEM((2, 4, 2, 8, wide), F32),
                pltpu.VMEM((2, TALL + 1, 2, 8, wide), F32),
                pltpu.VMEM((2, TALL, 2, 8, wide), F32),
                pltpu.VMEM((ROWS, ndate, 16, cols), BF16),
                pltpu.VMEM((ROWS, ndate, 16, cols), BF16),
                pltpu.VMEM((ROWS, 4 * ROWS, cols), BF16),
                pltpu.VMEM((4 * ROWS, 256), F32),
                pltpu.VMEM((3, ROWS, 256), F32),
                pltpu.SemaphoreType.DMA((ROWS, 3)),
                pltpu.SemaphoreType.DMA((2,)),
                pltpu.SemaphoreType.DMA((2,)),
                pltpu.SemaphoreType.DMA,
                pltpu.SemaphoreType.DMA((ROWS,)),
                pltpu.SemaphoreType.DMA((ROWS,)),
                pltpu.SemaphoreType.DMA((3,)),
                pltpu.SemaphoreType.DMA((3,)),
            ],
            compiler_params=pltpu.CompilerParams(
                collective_id=0, has_side_effects=True, vmem_limit_bytes=56 * 1024 * 1024
            ),
        )(backscatter, edge_dirs, labels, parcel_slot.reshape(-1, 128), jnp.asarray(basis))

    return jax.shard_map(
        local,
        mesh=mesh,
        in_specs=(P("date", None, "space", None), P("date", "space", None), P("space", "date"), P()),
        out_specs=(P("space", "date", None), P(("date", "space"), None)),
        check_vma=False,
    )
```

time: 1470 us -> 48.6 us (0.03)
  the two profiles are of different devices: /device:TPU:0 before, /device:TPU:112 now
where the time goes in v1:
time: 48.6 us; the launch traced here: 48.4 us
  Pallas kernels  44.8 us (92%)
  local copies, waits for them, and re-layouts  2.9 us (6%)
  between operations  0.65 us (1%)
    pallas_call x1, Pallas kernels, local(): pl.pallas_call(functools.partial(kernel, ndate, nspace, wide), out_shape=...  44.8 us
    unnamed x4, local copies, waits for them, and re-layouts  2.9 us

profile of v1, /device:TPU:112, one launch (start us, length us, event | category | flops | bytes accessed | tf_op | source)
XLA Modules:
  0.0 48.4 jit_solution(7327476444271066074)
XLA Ops:
  0.6 44.8 %shard_map.68 = (bf16[16,256,128]{2,1,0:T(8,128)(2,1)}, f32[16,128]{1,0:T(8,128)}) custom-call(f32[8,2,16,2048]{3,2,1,0:T(8,128)} %x_hbm.1, s32[8,16,2048]{2,1,0:T(8,128)} %e_hbm.1, s32[16,256]{1,0:T(8,128)} %labels_ref.1, s32[32,128]{1,0:T(8,128)} %bitcast.1, bf16[128,128]{1,0:T(8,128)(2,1)} %constant.2.clone.basis_ref), custom_call_target="tpu_custom_call" | custom-call | tf_op jit(solution)/shard_map/pallas_call | solution.py:325
  45.4 0.0 copy-start
  45.5 2.3 %copy.9 = bf16[16,256,128]{2,1,0:T(8,128)(2,1)} copy(bf16[16,256,128]{2,1,0:T(8,128)(2,1)} %get-tuple-element.4) | data formatting | bytes 2097152
  47.8 0.0 copy-done
  47.8 0.6 %copy.10 = f32[16,128]{1,0:T(8,128)} copy(f32[16,128]{1,0:T(8,128)S(1)} %copy-done) | data formatting | bytes 16384
Async XLA Ops:
  45.4 2.3 %copy-start = (f32[16,128]{1,0:T(8,128)S(1)}, f32[16,128]{1,0:T(8,128)}, u32[]{:S(2)}) copy-start(f32[16,128]{1,0:T(8,128)} %get-tuple-element.5) | copy-start | bytes 24580

commit v2 on v1

--- a/solution.py
+++ b/solution.py
@@ -17,6 +17,8 @@
 TALL = ROWS + 6
 ZERO = TALL
 LOG10E = 0.4342944819032518
+LEFT = 24
+TALLER = LEFT + 256 + 24
 
 
 def basis_table(dates, group, pols):
@@ -37,10 +39,9 @@
     ndate, nspace, wide,
     x_hbm, e_hbm, labels_ref, slot_ref, basis_ref,
     out_ref, means_ref,
-    xin, ein, a0, r7, xp, xm, d1, d2, vv, vm, tt, p2, hh, sendbuf, got, onehot, acc, qgot,
+    xin, ein, yy, a0, r7, c7, tt, vv, p2, hh, ey, sendbuf, got, onehot, acc, qgot,
     in_sem, halo_send, halo_recv, send_sem, recv_sem, own_sem, qsend, qrecv,
 ):
-    full = wide + 128
     date = lax.axis_index("date")
     space = lax.axis_index("space")
     half = ndate // 2
@@ -49,7 +50,7 @@
 
     def loads(r):
         for p in range(2):
-            yield pltpu.make_async_copy(x_hbm.at[:, p, r, :], xin.at[r + 3, p, :, 0:wide], in_sem.at[r, p])
+            yield pltpu.make_async_copy(x_hbm.at[:, p, r, :], xin.at[r + 3, p], in_sem.at[r, p])
         yield pltpu.make_async_copy(e_hbm.at[:, r, :], ein.at[r], in_sem.at[r, 2])
 
     for r in order:
@@ -71,14 +72,13 @@
     def _():
         pl.semaphore_signal(barrier, inc=1, device_id={"space": space + 1}, device_id_type=MESH)
 
-    xin[:, :, :, wide:] = jnp.zeros((TALL, 2, 8, 128), F32)
-    zero_row = jnp.zeros((2, 8, full), F32)
     for q in range(2):
-        a0[q, ZERO] = zero_row
-        r7[q, ZERO] = zero_row[:, :, :wide]
-        p2[q, ZERO] = zero_row[:, :, :wide]
-    xp[ZERO] = zero_row
-    xm[ZERO] = zero_row
+        for ref in (yy, a0, r7):
+            ref[q, ZERO] = jnp.zeros((TALLER, 128), F32)
+        p2[q, ZERO] = jnp.zeros((256, 128), F32)
+    yy[:, :, 0 : LEFT - 16, :] = jnp.zeros((2, TALL + 1, LEFT - 16, 128), F32)
+    yy[:, :, LEFT + 272 :, :] = jnp.zeros((2, TALL + 1, TALLER - LEFT - 272, 128), F32)
+    a0[:, :, 0 : LEFT - 16, :] = jnp.zeros((2, TALL + 1, LEFT - 16, 128), F32)
 
     base_date = lax.rem(date, half)
     base_space = space - lax.rem(space, 2)
@@ -97,13 +97,13 @@
 
     def down():
         return pltpu.make_async_remote_copy(
-            src_ref=xin.at[ROWS : ROWS + 3, :, :, 0:wide], dst_ref=xin.at[0:3, :, :, 0:wide],
+            src_ref=xin.at[ROWS : ROWS + 3], dst_ref=xin.at[0:3],
             send_sem=halo_send.at[0], recv_sem=halo_recv.at[0],
             device_id={"space": space + 1}, device_id_type=MESH)
 
     def up():
         return pltpu.make_async_remote_copy(
-            src_ref=xin.at[3:6, :, :, 0:wide], dst_ref=xin.at[ROWS + 3 : ROWS + 6, :, :, 0:wide],
+            src_ref=xin.at[3:6], dst_ref=xin.at[ROWS + 3 : ROWS + 6],
             send_sem=halo_send.at[1], recv_sem=halo_recv.at[1],
             device_id={"space": space - 1}, device_id_type=MESH)
 
@@ -123,11 +123,11 @@
 
     @pl.when(space == 0)
     def _():
-        xin[0:3, :, :, 0:wide] = jnp.zeros((3, 2, 8, wide), F32)
+        xin[0:3] = jnp.zeros((3, 2, 8, wide), F32)
 
     @pl.when(space == nspace - 1)
     def _():
-        xin[ROWS + 3 : ROWS + 6, :, :, 0:wide] = jnp.zeros((3, 2, 8, wide), F32)
+        xin[ROWS + 3 : ROWS + 6] = jnp.zeros((3, 2, 8, wide), F32)
 
     def send(r):
         for k in range(1, ndate):
@@ -138,81 +138,115 @@
                 device_id={"date": peer}, device_id_type=MESH).start()
         pltpu.make_async_copy(sendbuf.at[r, date], got.at[r, date], own_sem.at[r]).start()
 
-    def left(v, n):
-        return pltpu.roll(v, full - n, axis=1)
-
-    def right(v, n):
-        return pltpu.roll(v, n, axis=1)
-
     def back(i, s, n):
         return jnp.where(i - n >= s, i - n, ZERO)
 
-    def phase1(i, s, fresh, emit):
+    lanes = lax.broadcasted_iota(jnp.int32, (16, 128), 1)
+    width = wide // ndate
+
+    def spread(i):
+        halves = []
+        for h in range(2):
+            tiles = [xin[i, p, :, b * width + h * 128 : b * width + (h + 1) * 128] for b in range(ndate) for p in range(2)]
+            half_row = jnp.concatenate(tiles, axis=0).T
+            yy[0, i, LEFT + h * 128 : LEFT + (h + 1) * 128] = half_row
+            halves.append(half_row)
+        before = pltpu.roll(halves[1][112:], 16, axis=1)
+        after = pltpu.roll(halves[0][:16], 112, axis=1)
+        yy[0, i, LEFT - 16 : LEFT] = jnp.where(lanes >= 16, before, 0.0)
+        yy[0, i, LEFT + 256 : LEFT + 272] = jnp.where(lanes < 112, after, 0.0)
+        for n in range(4):
+            at = slice(LEFT - 16 + n * 72, LEFT - 16 + (n + 1) * 72)
+            x = yy[0, i, at]
+            yy[1, i, at] = x * x
+        for q in range(2):
+            for n in range(4):
+                at = LEFT - 16 + n * 72
+                x = yy[q, i, at : at + 72]
+                four = (x + yy[q, i, at + 1 : at + 73]) + (yy[q, i, at + 2 : at + 74] + yy[q, i, at + 3 : at + 75])
+                a0[q, i, at : at + 72] = four
+                r7[q, i, at : at + 72] = four + a0[q, i, at - 3 : at + 69] - x
+
+    def columns(i, s):
         lo = back(i, s, 7)
         new = lax.rem(i, 2)
-        old = 1 - new
-        for p in range(2):
-            if fresh:
-                x = xin[i, p]
-                for q in range(2):
-                    v = x * x if q else x
-                    pair = v + left(v, 1)
-                    four = pair + left(pair, 2)
-                    a0[q, i, p] = four
-                    r7[q, i, p] = (four + right(four, 3) - v)[:, :wide]
-                xp[i, p] = left(x, 3)
-                xm[i, p] = right(x, 3)
-            for q in range(2):
-                def sq(v):
-                    return v * v if q else v
-
-                d1[new, q, p] = left(d1[old, q, p] - sq(xp[lo, p]), 1) + sq(xm[i, p])
-                d2[new, q, p] = right(d2[old, q, p] - sq(xm[lo, p]), 1) + sq(xp[i, p])
-                v = vv[q, p] + (a0[q, i, p] - a0[q, lo, p])
-                vv[q, p] = v
-                if emit:
-                    vm[q, p] = right(v, 3)[:, :wide]
-
-    def phase2(i, s, emit):
-        lo = back(i, s, 7)
+        for q in range(2):
+            for n in range(4):
+                at = slice(LEFT - 16 + n * 72, LEFT - 16 + (n + 1) * 72)
+                c7[new, q, at] = c7[1 - new, q, at] + (yy[q, i, at] - yy[q, lo, at])
+            for n in range(3):
+                at = slice(LEFT - 8 + n * 88, LEFT - 8 + (n + 1) * 88)
+                vv[q, at] = vv[q, at] + (a0[q, i, at] - a0[q, lo, at])
+
+    def rising(i, lo, q, at, size):
         new = lax.rem(i, 2)
         old = 1 - new
+        t1 = tt[old, q, 0, at + 1 : at + 1 + size] - c7[old, q, at + 4 : at + 4 + size] + r7[q, i, at : at + size]
+        t5 = tt[old, q, 2, at + 1 : at + 1 + size] - r7[q, lo, at + 1 : at + 1 + size] + c7[new, q, at - 3 : at - 3 + size]
+        tt[new, q, 0, at : at + size] = t1
+        tt[new, q, 2, at : at + size] = t5
+        return t1, t5
+
+    def falling(i, lo, q, at, size):
+        new = lax.rem(i, 2)
+        old = 1 - new
+        t3 = tt[old, q, 1, at - 1 : at - 1 + size] - r7[q, lo, at - 1 : at - 1 + size] + c7[new, q, at + 3 : at + 3 + size]
+        t7 = tt[old, q, 3, at - 1 : at - 1 + size] - c7[old, q, at - 4 : at - 4 + size] + r7[q, i, at : at + size]
+        tt[new, q, 1, at : at + size] = t3
+        tt[new, q, 3, at : at + size] = t7
+        return t3, t7
+
+    def refresh(i):
+        last = 1 - lax.rem(i, 2)
+        for q in range(2):
+            for k in (0, 2):
+                own = tt[last, q, k, LEFT + 256 : LEFT + 264]
+                other = pltpu.roll(tt[last, q, k, LEFT : LEFT + 8], 112, axis=1)
+                tt[last, q, k, LEFT + 256 : LEFT + 264] = jnp.where(lanes[:8] < 112, other, own)
+            for k in (1, 3):
+                own = tt[last, q, k, LEFT - 8 : LEFT]
+                other = pltpu.roll(tt[last, q, k, LEFT + 248 : LEFT + 256], 16, axis=1)
+                tt[last, q, k, LEFT - 8 : LEFT] = jnp.where(lanes[:8] >= 16, other, own)
+
+    size = 64
+
+    def windows(i, s, emit):
+        lo = back(i, s, 7)
         r = i - 6
-        for c in range(ndate):
-            width = wide // ndate
-            cols = slice(c * width, (c + 1) * width)
+        if emit:
+            for h in range(2):
+                tiles = [ein[r, :, b * width + h * 128 : b * width + (h + 1) * 128] for b in range(ndate) for p in range(2)]
+                ey[h * 128 : (h + 1) * 128] = jnp.concatenate(tiles, axis=0).T
+        for q in range(2):
+            rising(i, lo, q, LEFT + 256, 8)
+            falling(i, lo, q, LEFT - 8, 8)
+        levels = []
+        for n in range(256 // size):
+            at = LEFT + n * size
+            here = slice(at, at + size)
+            plain = slice(n * size, (n + 1) * size)
             if emit:
-                e = ein[r, :, cols]
-                b0 = ((e & 1) > 0)[None]
-                b1 = ((e & 2) > 0)[None]
-                b2 = ((e & 4) > 0)[None]
+                e = ey[plain]
+                b0 = (e & 1) > 0
+                b1 = (e & 2) > 0
+                b2 = e > 3
             sums = []
             for q in range(2):
-                rn = r7[q, i, :, :, cols]
-                ro = r7[q, lo, :, :, cols]
-                d1n, d1o = d1[new, q, :, :, cols], d1[old, q, :, :, cols]
-                d2n, d2o = d2[new, q, :, :, cols], d2[old, q, :, :, cols]
-                t1 = tt[q, 0, :, :, cols] - d1o + rn
-                t3 = tt[q, 1, :, :, cols] + d2n - ro
-                t5 = tt[q, 2, :, :, cols] + d1n - ro
-                t7 = tt[q, 3, :, :, cols] - d2o + rn
-                pr = rn + r7[q, back(i, s, 1), :, :, cols]
-                h = pr + p2[q, back(i, s, 2), :, :, cols]
-                tt[q, 0, :, :, cols] = t1
-                tt[q, 1, :, :, cols] = t3
-                tt[q, 2, :, :, cols] = t5
-                tt[q, 3, :, :, cols] = t7
-                p2[q, i, :, :, cols] = pr
-                hh[q, i, :, :, cols] = h
+                t1, t5 = rising(i, lo, q, at, size)
+                t3, t7 = falling(i, lo, q, at, size)
+                pair = r7[q, i, here] + r7[q, back(i, s, 1), here]
+                h = pair + p2[q, back(i, s, 2), plain]
+                p2[q, i, plain] = pair
+                hh[q, i, plain] = h
                 if emit:
-                    s02 = jnp.where(b1, vv[q, :, :, cols], h)
-                    s46 = jnp.where(b1, vm[q, :, :, cols], hh[q, i - 3, :, :, cols])
+                    s02 = jnp.where(b1, vv[q, here], h)
+                    s46 = jnp.where(b1, vv[q, at - 3 : at - 3 + size], hh[q, i - 3, plain])
                     s13 = jnp.where(b1, t3, t1)
                     s57 = jnp.where(b1, t7, t5)
                     sums.append(jnp.where(b2, jnp.where(b0, s57, s46), jnp.where(b0, s13, s02)))
             if emit:
                 first, second = sums
-                x = xin[i - 3, :, :, cols]
+                x = yy[0, i - 3, here]
                 mean = first * (1.0 / 28.0)
                 sq_mean = mean * mean
                 excess = jnp.maximum(second * (1.0 / 28.0) - 1.25 * sq_mean, 0.0)
@@ -220,12 +254,14 @@
                 inv = pl.reciprocal(under, approx=True)
                 inv = inv * (2.0 - under * inv)
                 filtered = mean + excess * inv * (x - mean)
-                level = jnp.log(filtered) * LOG10E
-                sendbuf[r, c] = level.reshape(2 * 8, width).astype(BF16)
+                levels.append(jnp.log(filtered) * LOG10E)
+        if emit:
+            for h in range(2):
+                part = jnp.concatenate(levels[h * 128 // size : (h + 1) * 128 // size], axis=0).T
+                sendbuf[r, :, :, h * 128 : (h + 1) * 128] = part.astype(BF16).reshape(ndate, 16, 128)
 
     def reset():
-        d1[...] = jnp.zeros(d1.shape, F32)
-        d2[...] = jnp.zeros(d2.shape, F32)
+        c7[...] = jnp.zeros(c7.shape, F32)
         vv[...] = jnp.zeros(vv.shape, F32)
         tt[...] = jnp.zeros(tt.shape, F32)
 
@@ -236,8 +272,15 @@
                 def _():
                     for copy in loads(i - 3):
                         copy.wait()
-            phase1(i, s, fresh, emit)
-            phase2(i, s, emit)
+            if fresh:
+                spread(i)
+
+            @pl.when(jnp.logical_and(lax.rem(i - s, 8) == 0, i > s))
+            def _():
+                refresh(i)
+
+            columns(i, s)
+            windows(i, s, emit)
             if emit:
                 send(i - 6)
             return carry
@@ -318,7 +361,6 @@
 
     def local(backscatter, edge_dirs, labels, parcel_slot):
         wide = backscatter.shape[3]
-        full = wide + 128
         cols = wide // ndate
         any_spec = pl.BlockSpec(memory_space=pl.ANY)
         vmem = pl.BlockSpec(memory_space=pltpu.VMEM)
@@ -331,19 +373,17 @@
             in_specs=[any_spec, any_spec, vmem, vmem, vmem],
             out_specs=(vmem, vmem),
             scratch_shapes=[
-                pltpu.VMEM((TALL, 2, 8, full), F32),
+                pltpu.VMEM((TALL, 2, 8, wide), F32),
                 pltpu.VMEM((ROWS, 8, wide), jnp.int32),
-                pltpu.VMEM((2, TALL + 1, 2, 8, full), F32),
-                pltpu.VMEM((2, TALL + 1, 2, 8, wide), F32),
-                pltpu.VMEM((TALL + 1, 2, 8, full), F32),
-                pltpu.VMEM((TALL + 1, 2, 8, full), F32),
-                pltpu.VMEM((2, 2, 2, 8, full), F32),
-                pltpu.VMEM((2, 2, 2, 8, full), F32),
-                pltpu.VMEM((2, 2, 8, full), F32),
-                pltpu.VMEM((2, 2, 8, wide), F32),
-                pltpu.VMEM((2, 4, 2, 8, wide), F32),
-                pltpu.VMEM((2, TALL + 1, 2, 8, wide), F32),
-                pltpu.VMEM((2, TALL, 2, 8, wide), F32),
+                pltpu.VMEM((2, TALL + 1, TALLER, 128), F32),
+                pltpu.VMEM((2, TALL + 1, TALLER, 128), F32),
+                pltpu.VMEM((2, TALL + 1, TALLER, 128), F32),
+                pltpu.VMEM((2, 2, TALLER, 128), F32),
+                pltpu.VMEM((2, 2, 4, TALLER, 128), F32),
+                pltpu.VMEM((2, TALLER, 128), F32),
+                pltpu.VMEM((2, TALL + 1, 256, 128), F32),
+                pltpu.VMEM((2, TALL, 256, 128), F32),
+                pltpu.VMEM((256, 128), jnp.int32),
                 pltpu.VMEM((ROWS, ndate, 16, cols), BF16),
                 pltpu.VMEM((ROWS, ndate, 16, cols), BF16),
                 pltpu.VMEM((ROWS, 4 * ROWS, cols), BF16),

time: 48.6 us -> 43.9 us (0.903)
  Pallas kernels: 44.8 us -> 40.1 us
    pallas_call x1, Pallas kernels: 44.8 us -> 40.1 us  [local(): pl.pallas_call(functools.partial(kernel, ndate, nspace, wide), out_shape=...]
where the time goes in v2:
time: 43.9 us; the launch traced here: 43.7 us
  Pallas kernels  40.1 us (91%)
  local copies, waits for them, and re-layouts  2.9 us (7%)
  between operations  0.65 us (1%)
    pallas_call x1, Pallas kernels, local(): pl.pallas_call(functools.partial(kernel, ndate, nspace, wide), out_shape=...  40.1 us
    unnamed x4, local copies, waits for them, and re-layouts  2.9 us

profile of v2, /device:TPU:112, one launch (start us, length us, event | category | flops | bytes accessed | tf_op | source)
XLA Modules:
  0.0 43.7 jit_solution(14103038317889104609)
XLA Ops:
  0.6 40.1 %shard_map.68 = (bf16[16,256,128]{2,1,0:T(8,128)(2,1)}, f32[16,128]{1,0:T(8,128)}) custom-call(f32[8,2,16,2048]{3,2,1,0:T(8,128)} %x_hbm.1, s32[8,16,2048]{2,1,0:T(8,128)} %e_hbm.1, s32[16,256]{1,0:T(8,128)} %labels_ref.1, s32[32,128]{1,0:T(8,128)} %bitcast.1, bf16[128,128]{1,0:T(8,128)(2,1)} %constant.2.clone.basis_ref), custom_call_target="tpu_custom_call" | custom-call | tf_op jit(solution)/shard_map/pallas_call | solution.py:367
  40.7 0.0 copy-start
  40.8 2.3 %copy.9 = bf16[16,256,128]{2,1,0:T(8,128)(2,1)} copy(bf16[16,256,128]{2,1,0:T(8,128)(2,1)} %get-tuple-element.4) | data formatting | bytes 2097152
  43.1 0.0 copy-done
  43.1 0.6 %copy.10 = f32[16,128]{1,0:T(8,128)} copy(f32[16,128]{1,0:T(8,128)S(1)} %copy-done) | data formatting | bytes 16384
Async XLA Ops:
  40.7 2.3 %copy-start = (f32[16,128]{1,0:T(8,128)S(1)}, f32[16,128]{1,0:T(8,128)}, u32[]{:S(2)}) copy-start(f32[16,128]{1,0:T(8,128)} %get-tuple-element.5) | copy-start | bytes 24580

commit v3 on v2

--- a/solution.py
+++ b/solution.py
@@ -15,7 +15,7 @@
 DATES = 64
 ROWS = 16
 TALL = ROWS + 6
-ZERO = TALL
+GROUP = 5
 LOG10E = 0.4342944819032518
 LEFT = 24
 TALLER = LEFT + 256 + 24
@@ -39,7 +39,7 @@
     ndate, nspace, wide,
     x_hbm, e_hbm, labels_ref, slot_ref, basis_ref,
     out_ref, means_ref,
-    xin, ein, yy, a0, r7, c7, tt, vv, p2, hh, ey, sendbuf, got, onehot, acc, qgot,
+    xin, ein, yy, a0, r7, dd, ff, ahead, behind, ey, sendbuf, got, onehot, acc, qgot,
     in_sem, halo_send, halo_recv, send_sem, recv_sem, own_sem, qsend, qrecv,
 ):
     date = lax.axis_index("date")
@@ -71,14 +71,6 @@
     @pl.when(space < nspace - 1)
     def _():
         pl.semaphore_signal(barrier, inc=1, device_id={"space": space + 1}, device_id_type=MESH)
-
-    for q in range(2):
-        for ref in (yy, a0, r7):
-            ref[q, ZERO] = jnp.zeros((TALLER, 128), F32)
-        p2[q, ZERO] = jnp.zeros((256, 128), F32)
-    yy[:, :, 0 : LEFT - 16, :] = jnp.zeros((2, TALL + 1, LEFT - 16, 128), F32)
-    yy[:, :, LEFT + 272 :, :] = jnp.zeros((2, TALL + 1, TALLER - LEFT - 272, 128), F32)
-    a0[:, :, 0 : LEFT - 16, :] = jnp.zeros((2, TALL + 1, LEFT - 16, 128), F32)
 
     base_date = lax.rem(date, half)
     base_space = space - lax.rem(space, 2)
@@ -137,9 +129,6 @@
                 send_sem=send_sem, recv_sem=recv_sem.at[r],
                 device_id={"date": peer}, device_id_type=MESH).start()
         pltpu.make_async_copy(sendbuf.at[r, date], got.at[r, date], own_sem.at[r]).start()
-
-    def back(i, s, n):
-        return jnp.where(i - n >= s, i - n, ZERO)
 
     lanes = lax.broadcasted_iota(jnp.int32, (16, 128), 1)
     width = wide // ndate
@@ -160,151 +149,185 @@
             x = yy[0, i, at]
             yy[1, i, at] = x * x
         for q in range(2):
+            for n in range(3):
+                at = LEFT - 8 + n * 88
+                four = (yy[q, i, at : at + 88] + yy[q, i, at + 1 : at + 89]) + (yy[q, i, at + 2 : at + 90] + yy[q, i, at + 3 : at + 91])
+                a0[q, i, n * 88 : (n + 1) * 88] = four
             for n in range(4):
-                at = LEFT - 16 + n * 72
-                x = yy[q, i, at : at + 72]
-                four = (x + yy[q, i, at + 1 : at + 73]) + (yy[q, i, at + 2 : at + 74] + yy[q, i, at + 3 : at + 75])
-                a0[q, i, at : at + 72] = four
-                r7[q, i, at : at + 72] = four + a0[q, i, at - 3 : at + 69] - x
-
-    def columns(i, s):
-        lo = back(i, s, 7)
-        new = lax.rem(i, 2)
-        for q in range(2):
-            for n in range(4):
-                at = slice(LEFT - 16 + n * 72, LEFT - 16 + (n + 1) * 72)
-                c7[new, q, at] = c7[1 - new, q, at] + (yy[q, i, at] - yy[q, lo, at])
-            for n in range(3):
-                at = slice(LEFT - 8 + n * 88, LEFT - 8 + (n + 1) * 88)
-                vv[q, at] = vv[q, at] + (a0[q, i, at] - a0[q, lo, at])
-
-    def rising(i, lo, q, at, size):
-        new = lax.rem(i, 2)
-        old = 1 - new
-        t1 = tt[old, q, 0, at + 1 : at + 1 + size] - c7[old, q, at + 4 : at + 4 + size] + r7[q, i, at : at + size]
-        t5 = tt[old, q, 2, at + 1 : at + 1 + size] - r7[q, lo, at + 1 : at + 1 + size] + c7[new, q, at - 3 : at - 3 + size]
-        tt[new, q, 0, at : at + size] = t1
-        tt[new, q, 2, at : at + size] = t5
-        return t1, t5
-
-    def falling(i, lo, q, at, size):
-        new = lax.rem(i, 2)
-        old = 1 - new
-        t3 = tt[old, q, 1, at - 1 : at - 1 + size] - r7[q, lo, at - 1 : at - 1 + size] + c7[new, q, at + 3 : at + 3 + size]
-        t7 = tt[old, q, 3, at - 1 : at - 1 + size] - c7[old, q, at - 4 : at - 4 + size] + r7[q, i, at : at + size]
-        tt[new, q, 1, at : at + size] = t3
-        tt[new, q, 3, at : at + size] = t7
-        return t3, t7
-
-    def refresh(i):
-        last = 1 - lax.rem(i, 2)
-        for q in range(2):
-            for k in (0, 2):
-                own = tt[last, q, k, LEFT + 256 : LEFT + 264]
-                other = pltpu.roll(tt[last, q, k, LEFT : LEFT + 8], 112, axis=1)
-                tt[last, q, k, LEFT + 256 : LEFT + 264] = jnp.where(lanes[:8] < 112, other, own)
-            for k in (1, 3):
-                own = tt[last, q, k, LEFT - 8 : LEFT]
-                other = pltpu.roll(tt[last, q, k, LEFT + 248 : LEFT + 256], 16, axis=1)
-                tt[last, q, k, LEFT - 8 : LEFT] = jnp.where(lanes[:8] >= 16, other, own)
-
-    size = 64
-
-    def windows(i, s, emit):
-        lo = back(i, s, 7)
-        r = i - 6
-        if emit:
-            for h in range(2):
-                tiles = [ein[r, :, b * width + h * 128 : b * width + (h + 1) * 128] for b in range(ndate) for p in range(2)]
-                ey[h * 128 : (h + 1) * 128] = jnp.concatenate(tiles, axis=0).T
-        for q in range(2):
-            rising(i, lo, q, LEFT + 256, 8)
-            falling(i, lo, q, LEFT - 8, 8)
-        levels = []
-        for n in range(256 // size):
-            at = LEFT + n * size
-            here = slice(at, at + size)
-            plain = slice(n * size, (n + 1) * size)
-            if emit:
-                e = ey[plain]
+                at = 64 * n
+                r7[q, i, at : at + 64] = a0[q, i, at + 8 : at + 72] + a0[q, i, at + 5 : at + 69] - yy[q, i, LEFT + at : LEFT + at + 64]
+
+    def diagonals(rows):
+        for n, r in enumerate(sorted(rows)):
+            for q in range(2):
+                for k in range(2):
+                    side = -1 if k == 0 else 1
+                    for m in range(3):
+                        at = LEFT - 8 * k + 88 * m
+
+                        def x(i, off):
+                            return yy[q, i, at + off : at + off + 88]
+
+                        if n == 0:
+                            total = x(r, -3 * side)
+                            for i in range(1, 7):
+                                total = total + x(r + i, (i - 3) * side)
+                        else:
+                            total = dd[n - 1, q, k, at - side : at - side + 88] - x(r - 1, -4 * side) + x(r + 6, 3 * side)
+                        dd[n, q, k, at : at + 88] = total
+
+    def windows(rows, init):
+        step = rows[1] - rows[0]
+
+        def tile(t, carry):
+            at = pl.multiple_of(t * 8, 8)
+            here = pl.ds(at, 8)
+            pairs, quads, state, cols = {}, {}, {}, {}
+
+            def x(q, i, off):
+                return yy[q, i, pl.ds(at + LEFT + off, 8), :]
+
+            def row(q, i):
+                return r7[q, i, here, :]
+
+            def pair(q, i):
+                if (q, i) not in pairs:
+                    pairs[q, i] = row(q, i) + row(q, i + 1)
+                return pairs[q, i]
+
+            def quad(q, i):
+                if (q, i) not in quads:
+                    quads[q, i] = pair(q, i) + pair(q, i + 2)
+                return quads[q, i]
+
+            def start(q, r):
+                total = [None] * 4
+                for k in range(-3, 4):
+                    i, m = r + 3 + k, abs(k)
+                    four, ruof = a0[q, i, pl.ds(at + 8, 8), :], a0[q, i, pl.ds(at + 5, 8), :]
+                    if m == 0:
+                        parts = (four, four, ruof, ruof)
+                    elif m == 1:
+                        mid = x(q, i, 0)
+                        parts = (four + x(q, i, -1), four - mid, ruof - mid, ruof + x(q, i, 1))
+                    elif m == 2:
+                        whole, low, high = row(q, i), x(q, i, -3), x(q, i, 3)
+                        parts = (whole - low, high + x(q, i, 2), low + x(q, i, -2), whole - high)
+                    else:
+                        whole = row(q, i)
+                        parts = (whole, x(q, i, 3), x(q, i, -3), whole)
+                    if k < 0:
+                        parts = (parts[1], parts[0], parts[3], parts[2])
+                    total = [p if t is None else t + p for t, p in zip(total, parts)]
+                return total
+
+            for n, r in enumerate(rows):
+                e = ey[n, here, :]
                 b0 = (e & 1) > 0
                 b1 = (e & 2) > 0
                 b2 = e > 3
-            sums = []
-            for q in range(2):
-                t1, t5 = rising(i, lo, q, at, size)
-                t3, t7 = falling(i, lo, q, at, size)
-                pair = r7[q, i, here] + r7[q, back(i, s, 1), here]
-                h = pair + p2[q, back(i, s, 2), plain]
-                p2[q, i, plain] = pair
-                hh[q, i, plain] = h
-                if emit:
-                    s02 = jnp.where(b1, vv[q, here], h)
-                    s46 = jnp.where(b1, vv[q, at - 3 : at - 3 + size], hh[q, i - 3, plain])
+                for q in range(2):
+                    slot = sorted(rows).index(r)
+                    d1 = dd[slot, q, 0, pl.ds(at + LEFT, 8), :]
+                    d2 = dd[slot, q, 1, pl.ds(at + LEFT, 8), :]
+                    if n == 0 and init:
+                        t1, t3, t5, t7 = start(q, r)
+                        for k, value in enumerate((t1, t3 - d2, t5 - d1, t7)):
+                            behind[q, k, here, :] = value
+                        state[q] = (t1 - d1, t3, t5, t7 - d2)
+                    else:
+                        if n == 0:
+                            state[q] = [(ahead if step > 0 else behind)[q, k, here, :] for k in range(4)]
+                        t1, t3, t5, t7 = state[q]
+                        if step > 0:
+                            new, old = row(q, r + 6), row(q, r - 1)
+                            t1, t7 = t1 + new, t7 + new
+                            t3, t5 = t3 + d2 - old, t5 + d1 - old
+                            state[q] = (t1 - d1, t3, t5, t7 - d2)
+                        else:
+                            new, old = row(q, r), row(q, r + 7)
+                            t3, t5 = t3 + new, t5 + new
+                            t1, t7 = t1 + d1 - old, t7 + d2 - old
+                            state[q] = (t1, t3 - d2, t5 - d1, t7)
+                    if n == 0:
+                        both = []
+                        for off in (8, 5):
+                            total = a0[q, r, pl.ds(at + off, 8), :]
+                            for i in range(1, 7):
+                                total = total + a0[q, r + i, pl.ds(at + off, 8), :]
+                            both.append(total)
+                    else:
+                        new, old = (r + 6, r - 1) if step > 0 else (r, r + 7)
+                        both = [
+                            total + a0[q, new, pl.ds(at + off, 8), :] - a0[q, old, pl.ds(at + off, 8), :]
+                            for total, off in zip(cols[q], (8, 5))
+                        ]
+                    cols[q] = both
+                    s02 = jnp.where(b1, both[0], quad(q, r + 3))
+                    s46 = jnp.where(b1, both[1], quad(q, r))
                     s13 = jnp.where(b1, t3, t1)
                     s57 = jnp.where(b1, t7, t5)
-                    sums.append(jnp.where(b2, jnp.where(b0, s57, s46), jnp.where(b0, s13, s02)))
-            if emit:
-                first, second = sums
-                x = yy[0, i - 3, here]
-                mean = first * (1.0 / 28.0)
+                    ff[n, q, here, :] = jnp.where(b2, jnp.where(b0, s57, s46), jnp.where(b0, s13, s02))
+            if step > 0:
+                for q in range(2):
+                    for k in range(4):
+                        ahead[q, k, here, :] = state[q][k]
+            return carry
+
+        lax.fori_loop(0, 32, tile, 0)
+
+    def group(rows, init=False):
+        for n, r in enumerate(rows):
+            for h in range(2):
+                tiles = [ein[r, :, b * width + h * 128 : b * width + (h + 1) * 128] for b in range(ndate) for p in range(2)]
+                ey[n, h * 128 : (h + 1) * 128] = jnp.concatenate(tiles, axis=0).T
+        diagonals(rows)
+        windows(rows, init)
+        for n, r in enumerate(rows):
+            for h in range(2):
+                half_row = slice(h * 128, (h + 1) * 128)
+                x = yy[0, r + 3, LEFT + h * 128 : LEFT + (h + 1) * 128]
+                mean = ff[n, 0, half_row] * (1.0 / 28.0)
                 sq_mean = mean * mean
-                excess = jnp.maximum(second * (1.0 / 28.0) - 1.25 * sq_mean, 0.0)
+                excess = jnp.maximum(ff[n, 1, half_row] * (1.0 / 28.0) - 1.25 * sq_mean, 0.0)
                 under = excess + 0.3125 * sq_mean
                 inv = pl.reciprocal(under, approx=True)
                 inv = inv * (2.0 - under * inv)
                 filtered = mean + excess * inv * (x - mean)
-                levels.append(jnp.log(filtered) * LOG10E)
-        if emit:
-            for h in range(2):
-                part = jnp.concatenate(levels[h * 128 // size : (h + 1) * 128 // size], axis=0).T
-                sendbuf[r, :, :, h * 128 : (h + 1) * 128] = part.astype(BF16).reshape(ndate, 16, 128)
-
-    def reset():
-        c7[...] = jnp.zeros(c7.shape, F32)
-        vv[...] = jnp.zeros(vv.shape, F32)
-        tt[...] = jnp.zeros(tt.shape, F32)
-
-    def step(s, fresh, emit):
+                level = (jnp.log(filtered) * LOG10E).T
+                sendbuf[r, :, :, half_row] = level.astype(BF16).reshape(ndate, 16, 128)
+            send(r)
+
+    def spread_step(waits):
         def body(i, carry):
-            if fresh and s == 3:
+            if waits:
                 @pl.when(jnp.logical_and(i >= 6, i < ROWS))
                 def _():
                     for copy in loads(i - 3):
                         copy.wait()
-            if fresh:
-                spread(i)
-
-            @pl.when(jnp.logical_and(lax.rem(i - s, 8) == 0, i > s))
-            def _():
-                refresh(i)
-
-            columns(i, s)
-            windows(i, s, emit)
-            if emit:
-                send(i - 6)
+            spread(i)
             return carry
 
         return body
 
-    reset()
-    lax.fori_loop(3, 9, step(3, True, False), 0)
-    lax.fori_loop(9, ROWS + 3, step(3, True, True), 0)
+    lax.fori_loop(3, 14, spread_step(True), 0)
+    group([3, 4, 5, 6, 7], init=True)
+    lax.fori_loop(14, ROWS + 3, spread_step(True), 0)
+    group([8, 9, 10, 11, 12])
 
     @pl.when(space < nspace - 1)
     def _():
         up().wait_recv()
 
-    lax.fori_loop(ROWS + 3, ROWS + 6, step(3, True, True), 0)
+    lax.fori_loop(ROWS + 3, ROWS + 6, spread_step(False), 0)
+    group([13, 14, 15])
 
     @pl.when(space > 0)
     def _():
         down().wait_recv()
 
-    reset()
-    lax.fori_loop(0, 3, step(0, True, False), 0)
-    lax.fori_loop(3, 6, step(0, False, False), 0)
-    lax.fori_loop(6, 9, step(0, False, True), 0)
+    lax.fori_loop(0, 3, spread_step(False), 0)
+    group([2, 1, 0])
 
     acc[...] = jnp.zeros(acc.shape, F32)
     ones = jnp.ones((wide // ndate, 128), BF16)
@@ -318,11 +341,13 @@
         out_ref[r] = coeffs
         acc[...] += jnp.dot(onehot[r], jnp.concatenate([coeffs, ones], axis=1), preferred_element_type=F32)
 
-    def fit_step(n, carry):
-        fit(lax.rem(n + 3, ROWS))
+    def fit_step(m, carry):
+        for k in range(4):
+            n = 4 * m + k
+            fit(jnp.where(n < ROWS - 3, n + 3, ROWS - 1 - n))
         return carry
 
-    lax.fori_loop(0, ROWS, fit_step, 0)
+    lax.fori_loop(0, ROWS // 4, fit_step, 0)
 
     high = date // half
     low = lax.rem(space, 2)
@@ -375,15 +400,14 @@
             scratch_shapes=[
                 pltpu.VMEM((TALL, 2, 8, wide), F32),
                 pltpu.VMEM((ROWS, 8, wide), jnp.int32),
-                pltpu.VMEM((2, TALL + 1, TALLER, 128), F32),
-                pltpu.VMEM((2, TALL + 1, TALLER, 128), F32),
-                pltpu.VMEM((2, TALL + 1, TALLER, 128), F32),
-                pltpu.VMEM((2, 2, TALLER, 128), F32),
-                pltpu.VMEM((2, 2, 4, TALLER, 128), F32),
-                pltpu.VMEM((2, TALLER, 128), F32),
-                pltpu.VMEM((2, TALL + 1, 256, 128), F32),
+                pltpu.VMEM((2, TALL, TALLER, 128), F32),
+                pltpu.VMEM((2, TALL, 264, 128), F32),
                 pltpu.VMEM((2, TALL, 256, 128), F32),
-                pltpu.VMEM((256, 128), jnp.int32),
+                pltpu.VMEM((GROUP, 2, 2, TALLER, 128), F32),
+                pltpu.VMEM((GROUP, 2, 256, 128), F32),
+                pltpu.VMEM((2, 4, 256, 128), F32),
+                pltpu.VMEM((2, 4, 256, 128), F32),
+                pltpu.VMEM((GROUP, 256, 128), jnp.int32),
                 pltpu.VMEM((ROWS, ndate, 16, cols), BF16),
                 pltpu.VMEM((ROWS, ndate, 16, cols), BF16),
                 pltpu.VMEM((ROWS, 4 * ROWS, cols), BF16),

time: 43.9 us -> 36.4 us (0.83)
  Pallas kernels: 40.1 us -> 32.6 us
    pallas_call x1, Pallas kernels: 40.1 us -> 32.6 us  [local(): pl.pallas_call(functools.partial(kernel, ndate, nspace, wide), out_shape=...]
where the time goes in v3:
time: 36.4 us; the launch traced here: 36.2 us
  Pallas kernels  32.6 us (90%)
  local copies, waits for them, and re-layouts  2.9 us (8%)
  between operations  0.65 us (2%)
    pallas_call x1, Pallas kernels, local(): pl.pallas_call(functools.partial(kernel, ndate, nspace, wide), out_shape=...  32.6 us
    unnamed x4, local copies, waits for them, and re-layouts  2.9 us

profile of v3, /device:TPU:112, one launch (start us, length us, event | category | flops | bytes accessed | tf_op | source)
XLA Modules:
  0.0 36.2 jit_solution(14466044798425821008)
XLA Ops:
  0.6 32.6 %shard_map.68 = (bf16[16,256,128]{2,1,0:T(8,128)(2,1)}, f32[16,128]{1,0:T(8,128)}) custom-call(f32[8,2,16,2048]{3,2,1,0:T(8,128)} %x_hbm.1, s32[8,16,2048]{2,1,0:T(8,128)} %e_hbm.1, s32[16,256]{1,0:T(8,128)} %labels_ref.1, s32[32,128]{1,0:T(8,128)} %bitcast.1, bf16[128,128]{1,0:T(8,128)(2,1)} %constant.2.clone.basis_ref), custom_call_target="tpu_custom_call" | custom-call | tf_op jit(solution)/shard_map/pallas_call | solution.py:392
  33.3 0.0 copy-start
  33.3 2.3 %copy.9 = bf16[16,256,128]{2,1,0:T(8,128)(2,1)} copy(bf16[16,256,128]{2,1,0:T(8,128)(2,1)} %get-tuple-element.4) | data formatting | bytes 2097152
  35.6 0.0 copy-done
  35.6 0.6 %copy.10 = f32[16,128]{1,0:T(8,128)} copy(f32[16,128]{1,0:T(8,128)S(1)} %copy-done) | data formatting | bytes 16384
Async XLA Ops:
  33.3 2.3 %copy-start = (f32[16,128]{1,0:T(8,128)S(1)}, f32[16,128]{1,0:T(8,128)}, u32[]{:S(2)}) copy-start(f32[16,128]{1,0:T(8,128)} %get-tuple-element.5) | copy-start | bytes 24580

commit v4 on v3

--- a/solution.py
+++ b/solution.py
@@ -15,7 +15,8 @@
 DATES = 64
 ROWS = 16
 TALL = ROWS + 6
-GROUP = 5
+GROUP = 4
+LATE = (10, 11, 12, 13, 14, 15, 2, 1, 0)
 LOG10E = 0.4342944819032518
 LEFT = 24
 TALLER = LEFT + 256 + 24
@@ -37,10 +38,10 @@
 
 def kernel(
     ndate, nspace, wide,
-    x_hbm, e_hbm, labels_ref, slot_ref, basis_ref,
+    x_hbm, e_hbm, labels_hbm, slot_hbm, basis_hbm,
     out_ref, means_ref,
-    xin, ein, yy, a0, r7, dd, ff, ahead, behind, ey, sendbuf, got, onehot, acc, qgot,
-    in_sem, halo_send, halo_recv, send_sem, recv_sem, own_sem, qsend, qrecv,
+    xin, ein, yy, a0, r7, dd, ff, ahead, behind, ey, sendbuf, got, onehot, acc, qgot, labels_ref, slot_ref, basis_ref,
+    in_sem, small_sem, halo_send, halo_recv, send_sem, recv_sem, own_sem, qsend, qrecv,
 ):
     date = lax.axis_index("date")
     space = lax.axis_index("space")
@@ -53,6 +54,13 @@
             yield pltpu.make_async_copy(x_hbm.at[:, p, r, :], xin.at[r + 3, p], in_sem.at[r, p])
         yield pltpu.make_async_copy(e_hbm.at[:, r, :], ein.at[r], in_sem.at[r, 2])
 
+    small = [
+        pltpu.make_async_copy(source, target, small_sem.at[n])
+        for n, (source, target) in enumerate(
+            ((slot_hbm, slot_ref), (labels_hbm, labels_ref), (basis_hbm, basis_ref)))
+    ]
+    for copy in small:
+        copy.start()
     for r in order:
         for copy in loads(r):
             copy.start()
@@ -71,6 +79,9 @@
     @pl.when(space < nspace - 1)
     def _():
         pl.semaphore_signal(barrier, inc=1, device_id={"space": space + 1}, device_id_type=MESH)
+
+    for copy in small:
+        copy.wait()
 
     base_date = lax.rem(date, half)
     base_space = space - lax.rem(space, 2)
@@ -87,6 +98,12 @@
     for r in range(ROWS):
         onehot[r] = jnp.where(parcel_of == labels_ref[r : r + 1, :], 1.0, 0.0).astype(BF16)
 
+    present = onehot[0].astype(F32)
+    for r in range(1, ROWS):
+        present = present + onehot[r].astype(F32)
+    acc[:, :128] = jnp.zeros((4 * ROWS, 128), F32)
+    acc[:, 128:] = jnp.broadcast_to(jnp.sum(present, axis=1, keepdims=True), (4 * ROWS, 128))
+
     def down():
         return pltpu.make_async_remote_copy(
             src_ref=xin.at[ROWS : ROWS + 3], dst_ref=xin.at[0:3],
@@ -144,18 +161,23 @@
         after = pltpu.roll(halves[0][:16], 112, axis=1)
         yy[0, i, LEFT - 16 : LEFT] = jnp.where(lanes >= 16, before, 0.0)
         yy[0, i, LEFT + 256 : LEFT + 272] = jnp.where(lanes < 112, after, 0.0)
+        for at, size in ((LEFT - 16, 8), (LEFT + 256, 16)):
+            x = yy[0, i, at : at + size]
+            yy[1, i, at : at + size] = x * x
         for n in range(4):
-            at = slice(LEFT - 16 + n * 72, LEFT - 16 + (n + 1) * 72)
-            x = yy[0, i, at]
-            yy[1, i, at] = x * x
-        for q in range(2):
-            for n in range(3):
-                at = LEFT - 8 + n * 88
-                four = (yy[q, i, at : at + 88] + yy[q, i, at + 1 : at + 89]) + (yy[q, i, at + 2 : at + 90] + yy[q, i, at + 3 : at + 91])
-                a0[q, i, n * 88 : (n + 1) * 88] = four
-            for n in range(4):
-                at = 64 * n
-                r7[q, i, at : at + 64] = a0[q, i, at + 8 : at + 72] + a0[q, i, at + 5 : at + 69] - yy[q, i, LEFT + at : LEFT + at + 64]
+            start, size = (0, 72) if n == 0 else (8 + 64 * n, 64)
+            at = LEFT - 8 + start
+            shifted = [yy[0, i, at + k : at + k + size] for k in range(4)]
+            for q in range(2):
+                if q:
+                    shifted = [x * x for x in shifted]
+                    yy[1, i, at : at + size] = shifted[0]
+                four = (shifted[0] + shifted[1]) + (shifted[2] + shifted[3])
+                a0[q, i, start : start + size] = four
+                skip = 8 if n == 0 else 0
+                r7[q, i, 64 * n : 64 * n + 64] = (
+                    four[skip:] + a0[q, i, start + skip - 3 : start + size - 3] - shifted[0][skip:]
+                )
 
     def diagonals(rows):
         for n, r in enumerate(sorted(rows)):
@@ -274,7 +296,7 @@
                         ahead[q, k, here, :] = state[q][k]
             return carry
 
-        lax.fori_loop(0, 32, tile, 0)
+        lax.fori_loop(0, 16, lambda t, carry: tile(2 * t + 1, tile(2 * t, carry)), 0)
 
     def group(rows, init=False):
         for n, r in enumerate(rows):
@@ -292,7 +314,6 @@
                 excess = jnp.maximum(ff[n, 1, half_row] * (1.0 / 28.0) - 1.25 * sq_mean, 0.0)
                 under = excess + 0.3125 * sq_mean
                 inv = pl.reciprocal(under, approx=True)
-                inv = inv * (2.0 - under * inv)
                 filtered = mean + excess * inv * (x - mean)
                 level = (jnp.log(filtered) * LOG10E).T
                 sendbuf[r, :, :, half_row] = level.astype(BF16).reshape(ndate, 16, 128)
@@ -310,10 +331,31 @@
 
         return body
 
-    lax.fori_loop(3, 14, spread_step(True), 0)
-    group([3, 4, 5, 6, 7], init=True)
-    lax.fori_loop(14, ROWS + 3, spread_step(True), 0)
-    group([8, 9, 10, 11, 12])
+    def fit(r):
+        series = got[r].reshape(ndate * 16, width)
+        coeffs = lax.dot_general(series, basis_ref[...], (((0,), (0,)), ((), ())), preferred_element_type=F32)
+        out_ref[r] = coeffs.astype(BF16)
+
+    def take(rows):
+        for r in rows:
+            pltpu.make_async_copy(got.at[r, 0 : ndate - 1], got.at[r, 0 : ndate - 1], recv_sem.at[r]).wait()
+            pltpu.make_async_copy(sendbuf.at[r, date], got.at[r, date], own_sem.at[r]).wait()
+        total = acc[:, :128]
+        for r in rows:
+            series = got[r].reshape(ndate * 16, width)
+            total = total + lax.dot_general(onehot[r], series, (((1,), (1,)), ((), ())), preferred_element_type=F32)
+        acc[:, :128] = total
+        for r in rows:
+            if r not in LATE:
+                fit(r)
+
+    lax.fori_loop(3, 12, spread_step(True), 0)
+    group([3, 4, 5], init=True)
+    lax.fori_loop(12, 16, spread_step(True), 0)
+    group([6, 7, 8, 9])
+    lax.fori_loop(16, ROWS + 3, spread_step(True), 0)
+    group([10, 11, 12])
+    take(range(3, 6))
 
     @pl.when(space < nspace - 1)
     def _():
@@ -321,6 +363,7 @@
 
     lax.fori_loop(ROWS + 3, ROWS + 6, spread_step(False), 0)
     group([13, 14, 15])
+    take(range(6, 9))
 
     @pl.when(space > 0)
     def _():
@@ -328,26 +371,8 @@
 
     lax.fori_loop(0, 3, spread_step(False), 0)
     group([2, 1, 0])
-
-    acc[...] = jnp.zeros(acc.shape, F32)
-    ones = jnp.ones((wide // ndate, 128), BF16)
-
-    def fit(r):
-        pltpu.make_async_copy(got.at[r, 0 : ndate - 1], got.at[r, 0 : ndate - 1], recv_sem.at[r]).wait()
-        pltpu.make_async_copy(sendbuf.at[r, date], got.at[r, date], own_sem.at[r]).wait()
-        series = got[r].reshape(ndate * 16, wide // ndate)
-        coeffs = lax.dot_general(series, basis_ref[...], (((0,), (0,)), ((), ())), preferred_element_type=F32)
-        coeffs = coeffs.astype(BF16)
-        out_ref[r] = coeffs
-        acc[...] += jnp.dot(onehot[r], jnp.concatenate([coeffs, ones], axis=1), preferred_element_type=F32)
-
-    def fit_step(m, carry):
-        for k in range(4):
-            n = 4 * m + k
-            fit(jnp.where(n < ROWS - 3, n + 3, ROWS - 1 - n))
-        return carry
-
-    lax.fori_loop(0, ROWS // 4, fit_step, 0)
+    take(range(9, ROWS))
+    take(range(3))
 
     high = date // half
     low = lax.rem(space, 2)
@@ -361,11 +386,18 @@
             device_id={"date": opposite if far else date, "space": mate if near else space}, device_id_type=MESH)
         copy.start()
         copies.append(copy)
+
+    for r in LATE:
+        fit(r)
     total = acc[pl.ds(pl.multiple_of((high * 2 + low) * ROWS, ROWS), ROWS), :]
     for k, copy in enumerate(copies):
         copy.wait_recv()
         total = total + qgot[k]
-    means_ref[...] = total[:, :128] / jnp.maximum(total[:, 128:], 1.0)
+    sums, counts = total[:, :128], total[:, 128:]
+    coarse = sums.astype(BF16)
+    fine = (sums - coarse.astype(F32)).astype(BF16)
+    sums = jnp.dot(coarse, basis_ref[...], preferred_element_type=F32) + jnp.dot(fine, basis_ref[...], preferred_element_type=F32)
+    means_ref[...] = sums / jnp.maximum(counts, 1.0)
 
     for copy in copies:
         copy.wait_send()
@@ -387,7 +419,7 @@
     def local(backscatter, edge_dirs, labels, parcel_slot):
         wide = backscatter.shape[3]
         cols = wide // ndate
-        any_spec = pl.BlockSpec(memory_space=pl.ANY)
+        hbm = pl.BlockSpec(memory_space=pltpu.HBM)
         vmem = pl.BlockSpec(memory_space=pltpu.VMEM)
         return pl.pallas_call(
             functools.partial(kernel, ndate, nspace, wide),
@@ -395,7 +427,7 @@
                 jax.ShapeDtypeStruct((ROWS, cols, 128), BF16),
                 jax.ShapeDtypeStruct((ROWS, 128), F32),
             ),
-            in_specs=[any_spec, any_spec, vmem, vmem, vmem],
+            in_specs=[hbm] * 5,
             out_specs=(vmem, vmem),
             scratch_shapes=[
                 pltpu.VMEM((TALL, 2, 8, wide), F32),
@@ -413,7 +445,11 @@
                 pltpu.VMEM((ROWS, 4 * ROWS, cols), BF16),
                 pltpu.VMEM((4 * ROWS, 256), F32),
                 pltpu.VMEM((3, ROWS, 256), F32),
+                pltpu.VMEM(labels.shape, jnp.int32),
+                pltpu.VMEM((parcel_slot.shape[0] // 128, 128), jnp.int32),
+                pltpu.VMEM(basis.shape, BF16),
                 pltpu.SemaphoreType.DMA((ROWS, 3)),
+                pltpu.SemaphoreType.DMA((3,)),
                 pltpu.SemaphoreType.DMA((2,)),
                 pltpu.SemaphoreType.DMA((2,)),
                 pltpu.SemaphoreType.DMA,
@@ -423,9 +459,12 @@
                 pltpu.SemaphoreType.DMA((3,)),
             ],
             compiler_params=pltpu.CompilerParams(
-                collective_id=0, has_side_effects=True, vmem_limit_bytes=56 * 1024 * 1024
+                collective_id=0, has_side_effects=True, vmem_limit_bytes=52 * 1024 * 1024
             ),
-        )(backscatter, edge_dirs, labels, parcel_slot.reshape(-1, 128), jnp.asarray(basis))
+        )(*[
+            pltpu.with_memory_space_constraint(v, pltpu.HBM)
+            for v in (backscatter, edge_dirs, labels, parcel_slot.reshape(-1, 128), jnp.asarray(basis))
+        ])
 
     return jax.shard_map(
         local,

time: 36.4 us -> 33.4 us (0.918)
  Pallas kernels: 32.6 us -> 31 us
  local copies, waits for them, and re-layouts: 2.9 us -> 1.57 us
    pallas_call x1, Pallas kernels: 32.6 us -> 31 us  [local(): pl.pallas_call(functools.partial(kernel, ndate, nspace, wide), out_shape=...]
    unnamed x4 -> x2, local copies, waits for them, and re-layouts: 2.9 us -> 1.57 us
where the time goes in v4:
time: 33.4 us; the launch traced here: 33.2 us
  Pallas kernels  31 us (93%)
  local copies, waits for them, and re-layouts  1.57 us (5%)
  between operations  0.64 us (2%)
    pallas_call x1, Pallas kernels, local(): pl.pallas_call(functools.partial(kernel, ndate, nspace, wide), out_shape=...  31 us
    unnamed x2, local copies, waits for them, and re-layouts  1.57 us

profile of v4, /device:TPU:112, one launch (start us, length us, event | category | flops | bytes accessed | tf_op | source)
XLA Modules:
  0.0 33.2 jit_solution(147697709585393845)
XLA Ops:
  0.6 31.0 %shard_map.68 = (bf16[16,256,128]{2,1,0:T(8,128)(2,1)S(1)}, f32[16,128]{1,0:T(8,128)S(1)}) custom-call(f32[8,2,16,2048]{3,2,1,0:T(8,128)} %x_hbm.1, s32[8,16,2048]{2,1,0:T(8,128)} %e_hbm.1, s32[16,256]{1,0:T(8,128)} %labels_hbm.1, s32[32,128]{1,0:T(8,128)} %bitcast.1, bf16[128,128]{1,0:T(8,128)(2,1)} %constant.2.clone.basis_hbm), custom_call_target="tpu_custom_call" | custom-call | tf_op jit(solution)/shard_map/pallas_call | solution.py:424
  31.6 1.0 %copy.9 = bf16[16,256,128]{2,1,0:T(8,128)(2,1)} copy(bf16[16,256,128]{2,1,0:T(8,128)(2,1)S(1)} %get-tuple-element.4) | data formatting | bytes 2097152
  32.6 0.6 %copy.10 = f32[16,128]{1,0:T(8,128)} copy(f32[16,128]{1,0:T(8,128)S(1)} %get-tuple-element.5) | data formatting | bytes 16384

commit v5 on v4

--- a/solution.py
+++ b/solution.py
@@ -16,8 +16,9 @@
 ROWS = 16
 TALL = ROWS + 6
 GROUP = 4
-LATE = (10, 11, 12, 13, 14, 15, 2, 1, 0)
 LOG10E = 0.4342944819032518
+STEPS = 65535.0
+MIDDLE = 32768.0
 LEFT = 24
 TALLER = LEFT + 256 + 24
 
@@ -38,16 +39,16 @@
 
 def kernel(
     ndate, nspace, wide,
-    x_hbm, e_hbm, labels_hbm, slot_hbm, basis_hbm,
-    out_ref, means_ref,
-    xin, ein, yy, a0, r7, dd, ff, ahead, behind, ey, sendbuf, got, onehot, acc, qgot, labels_ref, slot_ref, basis_ref,
+    x_hbm, e_hbm, labels_hbm, slot_hbm,
+    got, total_ref,
+    xin, ein, yy, a0, r7, dd, ff, ahead, behind, ey, sendbuf, onehot, acc, qgot, labels_ref, slot_ref, edge_out, edge_in,
     in_sem, small_sem, halo_send, halo_recv, send_sem, recv_sem, own_sem, qsend, qrecv,
 ):
     date = lax.axis_index("date")
     space = lax.axis_index("space")
     half = ndate // 2
 
-    order = list(range(3)) + list(range(ROWS - 3, ROWS)) + list(range(3, ROWS - 3))
+    order = list(range(9)) + list(range(ROWS - 3, ROWS)) + list(range(9, ROWS - 3))
 
     def loads(r):
         for p in range(2):
@@ -57,7 +58,7 @@
     small = [
         pltpu.make_async_copy(source, target, small_sem.at[n])
         for n, (source, target) in enumerate(
-            ((slot_hbm, slot_ref), (labels_hbm, labels_ref), (basis_hbm, basis_ref)))
+            ((slot_hbm, slot_ref), (labels_hbm, labels_ref)))
     ]
     for copy in small:
         copy.start()
@@ -106,29 +107,42 @@
 
     def down():
         return pltpu.make_async_remote_copy(
-            src_ref=xin.at[ROWS : ROWS + 3], dst_ref=xin.at[0:3],
+            src_ref=edge_out.at[1], dst_ref=edge_in.at[0],
             send_sem=halo_send.at[0], recv_sem=halo_recv.at[0],
             device_id={"space": space + 1}, device_id_type=MESH)
 
     def up():
         return pltpu.make_async_remote_copy(
-            src_ref=xin.at[3:6], dst_ref=xin.at[ROWS + 3 : ROWS + 6],
+            src_ref=edge_out.at[0], dst_ref=edge_in.at[1],
             send_sem=halo_send.at[1], recv_sem=halo_recv.at[1],
             device_id={"space": space - 1}, device_id_type=MESH)
 
+    def pack(side, first):
+        for k in range(3):
+            x = xin[first + k].reshape(16, wide)
+            edge_out[side, k] = ((x * STEPS + 0.5).astype(jnp.int32) - 32768).astype(jnp.int16)
+
+    def unpack(side, first):
+        for k in range(3):
+            x = (edge_in[side, k].astype(jnp.int32).astype(F32) + MIDDLE) * (1.0 / STEPS)
+            xin[first + k] = x.reshape(2, 8, wide)
+
+    def halo_out():
+        for r in range(ROWS - 3, ROWS):
+            for copy in loads(r):
+                copy.wait()
+        pack(0, 3)
+        pack(1, ROWS)
+
+        @pl.when(space < nspace - 1)
+        def _():
+            down().start()
+
+        @pl.when(space > 0)
+        def _():
+            up().start()
+
     degree = (ndate - 1) + 1 + jnp.where(space > 0, 1, 0) + jnp.where(space < nspace - 1, 1, 0)
-    pl.semaphore_wait(barrier, degree)
-    for r in list(range(3)) + list(range(ROWS - 3, ROWS)):
-        for copy in loads(r):
-            copy.wait()
-
-    @pl.when(space < nspace - 1)
-    def _():
-        down().start()
-
-    @pl.when(space > 0)
-    def _():
-        up().start()
 
     @pl.when(space == 0)
     def _():
@@ -322,7 +336,7 @@
     def spread_step(waits):
         def body(i, carry):
             if waits:
-                @pl.when(jnp.logical_and(i >= 6, i < ROWS))
+                @pl.when(i < ROWS)
                 def _():
                     for copy in loads(i - 3):
                         copy.wait()
@@ -330,11 +344,6 @@
             return carry
 
         return body
-
-    def fit(r):
-        series = got[r].reshape(ndate * 16, width)
-        coeffs = lax.dot_general(series, basis_ref[...], (((0,), (0,)), ((), ())), preferred_element_type=F32)
-        out_ref[r] = coeffs.astype(BF16)
 
     def take(rows):
         for r in rows:
@@ -345,11 +354,10 @@
             series = got[r].reshape(ndate * 16, width)
             total = total + lax.dot_general(onehot[r], series, (((1,), (1,)), ((), ())), preferred_element_type=F32)
         acc[:, :128] = total
-        for r in rows:
-            if r not in LATE:
-                fit(r)
 
     lax.fori_loop(3, 12, spread_step(True), 0)
+    pl.semaphore_wait(barrier, degree)
+    halo_out()
     group([3, 4, 5], init=True)
     lax.fori_loop(12, 16, spread_step(True), 0)
     group([6, 7, 8, 9])
@@ -360,6 +368,7 @@
     @pl.when(space < nspace - 1)
     def _():
         up().wait_recv()
+        unpack(1, ROWS + 3)
 
     lax.fori_loop(ROWS + 3, ROWS + 6, spread_step(False), 0)
     group([13, 14, 15])
@@ -368,6 +377,7 @@
     @pl.when(space > 0)
     def _():
         down().wait_recv()
+        unpack(0, 0)
 
     lax.fori_loop(0, 3, spread_step(False), 0)
     group([2, 1, 0])
@@ -387,29 +397,41 @@
         copy.start()
         copies.append(copy)
 
-    for r in LATE:
-        fit(r)
     total = acc[pl.ds(pl.multiple_of((high * 2 + low) * ROWS, ROWS), ROWS), :]
     for k, copy in enumerate(copies):
         copy.wait_recv()
         total = total + qgot[k]
-    sums, counts = total[:, :128], total[:, 128:]
+    total_ref[...] = total
+
+    for copy in copies:
+        copy.wait_send()
+    pltpu.make_async_copy(sendbuf.at[:, 0 : ndate - 1], sendbuf.at[:, 0 : ndate - 1], send_sem).wait()
+
+    @pl.when(space < nspace - 1)
+    def _():
+        down().wait_send()
+
+    @pl.when(space > 0)
+    def _():
+        up().wait_send()
+
+
+def fit_kernel(got, total_ref, basis_ref, out_hbm, means_ref, out, out_sem):
+    def copy(r):
+        return pltpu.make_async_copy(out.at[r], out_hbm.at[r], out_sem.at[r])
+
+    for r in range(ROWS):
+        series = got[r].reshape(basis_ref.shape[0], got.shape[3])
+        coeffs = lax.dot_general(series, basis_ref[...], (((0,), (0,)), ((), ())), preferred_element_type=F32)
+        out[r] = coeffs.astype(BF16)
+        copy(r).start()
+    sums, counts = total_ref[:, :128], total_ref[:, 128:]
     coarse = sums.astype(BF16)
     fine = (sums - coarse.astype(F32)).astype(BF16)
     sums = jnp.dot(coarse, basis_ref[...], preferred_element_type=F32) + jnp.dot(fine, basis_ref[...], preferred_element_type=F32)
     means_ref[...] = sums / jnp.maximum(counts, 1.0)
-
-    for copy in copies:
-        copy.wait_send()
-    pltpu.make_async_copy(sendbuf.at[:, 0 : ndate - 1], sendbuf.at[:, 0 : ndate - 1], send_sem).wait()
-
-    @pl.when(space < nspace - 1)
-    def _():
-        down().wait_send()
-
-    @pl.when(space > 0)
-    def _():
-        up().wait_send()
+    for r in range(ROWS):
+        copy(r).wait()
 
 
 def solution(mesh):
@@ -421,13 +443,13 @@
         cols = wide // ndate
         hbm = pl.BlockSpec(memory_space=pltpu.HBM)
         vmem = pl.BlockSpec(memory_space=pltpu.VMEM)
-        return pl.pallas_call(
+        got, total = pl.pallas_call(
             functools.partial(kernel, ndate, nspace, wide),
             out_shape=(
-                jax.ShapeDtypeStruct((ROWS, cols, 128), BF16),
-                jax.ShapeDtypeStruct((ROWS, 128), F32),
+                jax.ShapeDtypeStruct((ROWS, ndate, 16, cols), BF16),
+                jax.ShapeDtypeStruct((ROWS, 256), F32),
             ),
-            in_specs=[hbm] * 5,
+            in_specs=[hbm] * 4,
             out_specs=(vmem, vmem),
             scratch_shapes=[
                 pltpu.VMEM((TALL, 2, 8, wide), F32),
@@ -441,15 +463,15 @@
                 pltpu.VMEM((2, 4, 256, 128), F32),
                 pltpu.VMEM((GROUP, 256, 128), jnp.int32),
                 pltpu.VMEM((ROWS, ndate, 16, cols), BF16),
-                pltpu.VMEM((ROWS, ndate, 16, cols), BF16),
                 pltpu.VMEM((ROWS, 4 * ROWS, cols), BF16),
                 pltpu.VMEM((4 * ROWS, 256), F32),
                 pltpu.VMEM((3, ROWS, 256), F32),
                 pltpu.VMEM(labels.shape, jnp.int32),
                 pltpu.VMEM((parcel_slot.shape[0] // 128, 128), jnp.int32),
-                pltpu.VMEM(basis.shape, BF16),
+                pltpu.VMEM((2, 3, 16, wide), jnp.int16),
+                pltpu.VMEM((2, 3, 16, wide), jnp.int16),
                 pltpu.SemaphoreType.DMA((ROWS, 3)),
-                pltpu.SemaphoreType.DMA((3,)),
+                pltpu.SemaphoreType.DMA((2,)),
                 pltpu.SemaphoreType.DMA((2,)),
                 pltpu.SemaphoreType.DMA((2,)),
                 pltpu.SemaphoreType.DMA,
@@ -459,12 +481,23 @@
                 pltpu.SemaphoreType.DMA((3,)),
             ],
             compiler_params=pltpu.CompilerParams(
-                collective_id=0, has_side_effects=True, vmem_limit_bytes=52 * 1024 * 1024
+                collective_id=0, has_side_effects=True, vmem_limit_bytes=44 * 1024 * 1024
             ),
         )(*[
             pltpu.with_memory_space_constraint(v, pltpu.HBM)
-            for v in (backscatter, edge_dirs, labels, parcel_slot.reshape(-1, 128), jnp.asarray(basis))
+            for v in (backscatter, edge_dirs, labels, parcel_slot.reshape(-1, 128))
         ])
+        return pl.pallas_call(
+            fit_kernel,
+            out_shape=(
+                jax.ShapeDtypeStruct((ROWS, cols, 128), BF16),
+                jax.ShapeDtypeStruct((ROWS, 128), F32),
+            ),
+            in_specs=[vmem] * 3,
+            out_specs=(hbm, vmem),
+            scratch_shapes=[pltpu.VMEM((ROWS, cols, 128), BF16), pltpu.SemaphoreType.DMA((ROWS,))],
+            compiler_params=pltpu.CompilerParams(vmem_limit_bytes=8 * 1024 * 1024),
+        )(got, total, jnp.asarray(basis))
 
     return jax.shard_map(
         local,

time: 33.4 us -> 30.3 us (0.907)
  the two profiles are of different devices: /device:TPU:112 before, /device:TPU:1 now
where the time goes in v5:
time: 30.3 us; the launch traced here: 30.2 us
  Pallas kernels  29.5 us (97%)
  between operations  0.65 us (2%)
    pallas_call x1, Pallas kernels, local(): pl.pallas_call(functools.partial(kernel, ndate, nspace, wide), out_shape=...  27.6 us
    pallas_call x1, Pallas kernels, local(): pl.pallas_call(fit_kernel, out_shape=(jax.ShapeDtypeStruct((ROWS, cols, 1...  1.92 us

profile of v5, /device:TPU:1, one launch (start us, length us, event | category | flops | bytes accessed | tf_op | source)
XLA Modules:
  0.0 30.2 jit_solution(15507781842083646966)
XLA Ops:
  0.6 0.0 copy-start
  0.6 27.6 %shard_map.68 = (bf16[16,8,16,256]{3,2,1,0:T(8,128)(2,1)S(1)}, f32[16,256]{1,0:T(8,128)S(1)}) custom-call(f32[8,2,16,2048]{3,2,1,0:T(8,128)} %x_hbm.1, s32[8,16,2048]{2,1,0:T(8,128)} %e_hbm.1, s32[16,256]{1,0:T(8,128)} %labels_hbm.1, s32[32,128]{1,0:T(8,128)} %bitcast.1), custom_call_target="tpu_custom_call" | custom-call | tf_op jit(solution)/shard_map/pallas_call | solution.py:446
  28.3 0.0 copy-done
  28.3 1.9 %shard_map.69 = (bf16[16,256,128]{2,1,0:T(8,128)(2,1)}, f32[16,128]{1,0:T(8,128)}) custom-call(bf16[16,8,16,256]{3,2,1,0:T(8,128)(2,1)S(1)} %get-tuple-element.4.got, f32[16,256]{1,0:T(8,128)S(1)} %get-tuple-element.5.total_ref, bf16[128,128]{1,0:T(8,128)(2,1)S(1)} %copy-done), custom_call_target="tpu_custom_call" | custom-call | tf_op jit(solution)/shard_map/pallas_call | solution.py:490
Async XLA Ops:
  0.6 27.6 %copy-start = (bf16[128,128]{1,0:T(8,128)(2,1)S(1)}, bf16[128,128]{1,0:T(8,128)(2,1)}, u32[]{:S(2)}) copy-start(bf16[128,128]{1,0:T(8,128)(2,1)} %constant.2.clone.basis_ref) | copy-start | bytes 98308

commit v6 on v5

--- a/solution.py
+++ b/solution.py
@@ -16,6 +16,7 @@
 ROWS = 16
 TALL = ROWS + 6
 GROUP = 4
+FAR_FIRST = (4, 3, 5, 2, 6, 1, 7)
 LOG10E = 0.4342944819032518
 STEPS = 65535.0
 MIDDLE = 32768.0
@@ -39,9 +40,9 @@
 
 def kernel(
     ndate, nspace, wide,
-    x_hbm, e_hbm, labels_hbm, slot_hbm,
-    got, total_ref,
-    xin, ein, yy, a0, r7, dd, ff, ahead, behind, ey, sendbuf, onehot, acc, qgot, labels_ref, slot_ref, edge_out, edge_in,
+    x_hbm, e_hbm, labels_hbm, slot_hbm, basis_hbm,
+    coeffs_ref, total_ref,
+    xin, ein, yy, a0, r7, dd, ff, ahead, behind, ey, sendbuf, got, onehot, acc, qgot, labels_ref, slot_ref, basis_ref, edge_out, edge_in,
     in_sem, small_sem, halo_send, halo_recv, send_sem, recv_sem, own_sem, qsend, qrecv,
 ):
     date = lax.axis_index("date")
@@ -58,7 +59,7 @@
     small = [
         pltpu.make_async_copy(source, target, small_sem.at[n])
         for n, (source, target) in enumerate(
-            ((slot_hbm, slot_ref), (labels_hbm, labels_ref)))
+            ((slot_hbm, slot_ref), (labels_hbm, labels_ref), (basis_hbm, basis_ref)))
     ]
     for copy in small:
         copy.start()
@@ -81,30 +82,6 @@
     def _():
         pl.semaphore_signal(barrier, inc=1, device_id={"space": space + 1}, device_id_type=MESH)
 
-    for copy in small:
-        copy.wait()
-
-    base_date = lax.rem(date, half)
-    base_space = space - lax.rem(space, 2)
-    parts = []
-    for u in range(4):
-        owner = (base_date + (u // 2) * half) * nspace + base_space + u % 2
-        parts.append(lax.broadcasted_iota(jnp.int32, (ROWS, 128), 0) + owner * ROWS)
-    ids = jnp.concatenate(parts, axis=0)
-    lane = lax.broadcasted_iota(jnp.int32, (4 * ROWS, 128), 1).astype(F32)
-    total = jnp.zeros((4 * ROWS, 128), F32)
-    for g in range(slot_ref.shape[0]):
-        total = total + jnp.where(ids == slot_ref[g : g + 1, :], lane + float(128 * g), 0.0)
-    parcel_of = jnp.sum(total, axis=1, keepdims=True).astype(jnp.int32)
-    for r in range(ROWS):
-        onehot[r] = jnp.where(parcel_of == labels_ref[r : r + 1, :], 1.0, 0.0).astype(BF16)
-
-    present = onehot[0].astype(F32)
-    for r in range(1, ROWS):
-        present = present + onehot[r].astype(F32)
-    acc[:, :128] = jnp.zeros((4 * ROWS, 128), F32)
-    acc[:, 128:] = jnp.broadcast_to(jnp.sum(present, axis=1, keepdims=True), (4 * ROWS, 128))
-
     def down():
         return pltpu.make_async_remote_copy(
             src_ref=edge_out.at[1], dst_ref=edge_in.at[0],
@@ -153,7 +130,7 @@
         xin[ROWS + 3 : ROWS + 6] = jnp.zeros((3, 2, 8, wide), F32)
 
     def send(r):
-        for k in range(1, ndate):
+        for k in FAR_FIRST:
             peer = lax.rem(date + k, ndate)
             pltpu.make_async_remote_copy(
                 src_ref=sendbuf.at[r, peer], dst_ref=got.at[r, date],
@@ -310,7 +287,7 @@
                         ahead[q, k, here, :] = state[q][k]
             return carry
 
-        lax.fori_loop(0, 16, lambda t, carry: tile(2 * t + 1, tile(2 * t, carry)), 0)
+        lax.fori_loop(0, 8, lambda t, c: tile(4 * t + 3, tile(4 * t + 2, tile(4 * t + 1, tile(4 * t, c)))), 0)
 
     def group(rows, init=False):
         for n, r in enumerate(rows):
@@ -329,8 +306,8 @@
                 under = excess + 0.3125 * sq_mean
                 inv = pl.reciprocal(under, approx=True)
                 filtered = mean + excess * inv * (x - mean)
-                level = (jnp.log(filtered) * LOG10E).T
-                sendbuf[r, :, :, half_row] = level.astype(BF16).reshape(ndate, 16, 128)
+                level = (jnp.log(filtered) * LOG10E).astype(BF16).T
+                sendbuf[r, :, :, half_row] = level.reshape(ndate, 16, 128)
             send(r)
 
     def spread_step(waits):
@@ -355,33 +332,56 @@
             total = total + lax.dot_general(onehot[r], series, (((1,), (1,)), ((), ())), preferred_element_type=F32)
         acc[:, :128] = total
 
-    lax.fori_loop(3, 12, spread_step(True), 0)
+    lax.fori_loop(3, 12, spread_step(True), 0, unroll=True)
     pl.semaphore_wait(barrier, degree)
     halo_out()
     group([3, 4, 5], init=True)
-    lax.fori_loop(12, 16, spread_step(True), 0)
+    lax.fori_loop(12, 16, spread_step(True), 0, unroll=True)
     group([6, 7, 8, 9])
-    lax.fori_loop(16, ROWS + 3, spread_step(True), 0)
+    lax.fori_loop(16, ROWS + 3, spread_step(True), 0, unroll=True)
     group([10, 11, 12])
-    take(range(3, 6))
 
     @pl.when(space < nspace - 1)
     def _():
         up().wait_recv()
         unpack(1, ROWS + 3)
 
-    lax.fori_loop(ROWS + 3, ROWS + 6, spread_step(False), 0)
+    lax.fori_loop(ROWS + 3, ROWS + 6, spread_step(False), 0, unroll=True)
     group([13, 14, 15])
-    take(range(6, 9))
 
     @pl.when(space > 0)
     def _():
         down().wait_recv()
         unpack(0, 0)
 
-    lax.fori_loop(0, 3, spread_step(False), 0)
+    lax.fori_loop(0, 3, spread_step(False), 0, unroll=True)
     group([2, 1, 0])
-    take(range(9, ROWS))
+
+    for copy in small:
+        copy.wait()
+
+    base_date = lax.rem(date, half)
+    base_space = space - lax.rem(space, 2)
+    parts = []
+    for u in range(4):
+        owner = (base_date + (u // 2) * half) * nspace + base_space + u % 2
+        parts.append(lax.broadcasted_iota(jnp.int32, (ROWS, 128), 0) + owner * ROWS)
+    ids = jnp.concatenate(parts, axis=0)
+    lane = lax.broadcasted_iota(jnp.int32, (4 * ROWS, 128), 1).astype(F32)
+    total = jnp.zeros((4 * ROWS, 128), F32)
+    for g in range(slot_ref.shape[0]):
+        total = total + jnp.where(ids == slot_ref[g : g + 1, :], lane + float(128 * g), 0.0)
+    parcel_of = jnp.sum(total, axis=1, keepdims=True).astype(jnp.int32)
+    for r in range(ROWS):
+        onehot[r] = jnp.where(parcel_of == labels_ref[r : r + 1, :], 1.0, 0.0).astype(BF16)
+
+    present = onehot[0].astype(F32)
+    for r in range(1, ROWS):
+        present = present + onehot[r].astype(F32)
+    acc[:, :128] = jnp.zeros((4 * ROWS, 128), F32)
+    acc[:, 128:] = jnp.broadcast_to(jnp.sum(present, axis=1, keepdims=True), (4 * ROWS, 128))
+
+    take(range(3, ROWS))
     take(range(3))
 
     high = date // half
@@ -397,6 +397,11 @@
         copy.start()
         copies.append(copy)
 
+    for r in range(ROWS):
+        series = got[r].reshape(ndate * 16, width)
+        coeffs = lax.dot_general(series, basis_ref[...], (((0,), (0,)), ((), ())), preferred_element_type=F32)
+        coeffs_ref[r] = coeffs.astype(BF16)
+
     total = acc[pl.ds(pl.multiple_of((high * 2 + low) * ROWS, ROWS), ROWS), :]
     for k, copy in enumerate(copies):
         copy.wait_recv()
@@ -416,22 +421,20 @@
         up().wait_send()
 
 
-def fit_kernel(got, total_ref, basis_ref, out_hbm, means_ref, out, out_sem):
-    def copy(r):
-        return pltpu.make_async_copy(out.at[r], out_hbm.at[r], out_sem.at[r])
-
-    for r in range(ROWS):
-        series = got[r].reshape(basis_ref.shape[0], got.shape[3])
-        coeffs = lax.dot_general(series, basis_ref[...], (((0,), (0,)), ((), ())), preferred_element_type=F32)
-        out[r] = coeffs.astype(BF16)
-        copy(r).start()
+def finish(coeffs_ref, total_ref, basis_ref, out_hbm, means_ref, out_sem):
+    copies = [
+        pltpu.make_async_copy(coeffs_ref.at[4 * n : 4 * n + 4], out_hbm.at[4 * n : 4 * n + 4], out_sem.at[n])
+        for n in range(ROWS // 4)
+    ]
+    for copy in copies:
+        copy.start()
     sums, counts = total_ref[:, :128], total_ref[:, 128:]
     coarse = sums.astype(BF16)
     fine = (sums - coarse.astype(F32)).astype(BF16)
     sums = jnp.dot(coarse, basis_ref[...], preferred_element_type=F32) + jnp.dot(fine, basis_ref[...], preferred_element_type=F32)
     means_ref[...] = sums / jnp.maximum(counts, 1.0)
-    for r in range(ROWS):
-        copy(r).wait()
+    for copy in copies:
+        copy.wait()
 
 
 def solution(mesh):
@@ -443,13 +446,13 @@
         cols = wide // ndate
         hbm = pl.BlockSpec(memory_space=pltpu.HBM)
         vmem = pl.BlockSpec(memory_space=pltpu.VMEM)
-        got, total = pl.pallas_call(
+        coeffs, total = pl.pallas_call(
             functools.partial(kernel, ndate, nspace, wide),
             out_shape=(
-                jax.ShapeDtypeStruct((ROWS, ndate, 16, cols), BF16),
+                jax.ShapeDtypeStruct((ROWS, cols, 128), BF16),
                 jax.ShapeDtypeStruct((ROWS, 256), F32),
             ),
-            in_specs=[hbm] * 4,
+            in_specs=[hbm] * 5,
             out_specs=(vmem, vmem),
             scratch_shapes=[
                 pltpu.VMEM((TALL, 2, 8, wide), F32),
@@ -463,15 +466,17 @@
                 pltpu.VMEM((2, 4, 256, 128), F32),
                 pltpu.VMEM((GROUP, 256, 128), jnp.int32),
                 pltpu.VMEM((ROWS, ndate, 16, cols), BF16),
+                pltpu.VMEM((ROWS, ndate, 16, cols), BF16),
                 pltpu.VMEM((ROWS, 4 * ROWS, cols), BF16),
                 pltpu.VMEM((4 * ROWS, 256), F32),
                 pltpu.VMEM((3, ROWS, 256), F32),
                 pltpu.VMEM(labels.shape, jnp.int32),
                 pltpu.VMEM((parcel_slot.shape[0] // 128, 128), jnp.int32),
+                pltpu.VMEM(basis.shape, BF16),
                 pltpu.VMEM((2, 3, 16, wide), jnp.int16),
                 pltpu.VMEM((2, 3, 16, wide), jnp.int16),
                 pltpu.SemaphoreType.DMA((ROWS, 3)),
-                pltpu.SemaphoreType.DMA((2,)),
+                pltpu.SemaphoreType.DMA((3,)),
                 pltpu.SemaphoreType.DMA((2,)),
                 pltpu.SemaphoreType.DMA((2,)),
                 pltpu.SemaphoreType.DMA,
@@ -485,19 +490,19 @@
             ),
         )(*[
             pltpu.with_memory_space_constraint(v, pltpu.HBM)
-            for v in (backscatter, edge_dirs, labels, parcel_slot.reshape(-1, 128))
+            for v in (backscatter, edge_dirs, labels, parcel_slot.reshape(-1, 128), jnp.asarray(basis))
         ])
         return pl.pallas_call(
-            fit_kernel,
+            finish,
             out_shape=(
                 jax.ShapeDtypeStruct((ROWS, cols, 128), BF16),
                 jax.ShapeDtypeStruct((ROWS, 128), F32),
             ),
             in_specs=[vmem] * 3,
             out_specs=(hbm, vmem),
-            scratch_shapes=[pltpu.VMEM((ROWS, cols, 128), BF16), pltpu.SemaphoreType.DMA((ROWS,))],
+            scratch_shapes=[pltpu.SemaphoreType.DMA((ROWS // 4,))],
             compiler_params=pltpu.CompilerParams(vmem_limit_bytes=8 * 1024 * 1024),
-        )(got, total, jnp.asarray(basis))
+        )(coeffs, total, jnp.asarray(basis))
 
     return jax.shard_map(
         local,

time: 30.3 us -> 28.6 us (0.944)
  the two profiles are of different devices: /device:TPU:1 before, /device:TPU:112 now
where the time goes in v6:
time: 28.6 us; the launch traced here: 28 us
  Pallas kernels  27.3 us (95%)
  between operations  0.65 us (2%)
    pallas_call x1, Pallas kernels, local(): pl.pallas_call(functools.partial(kernel, ndate, nspace, wide), out_shape=...  25.7 us
    pallas_call x1, Pallas kernels, local(): pl.pallas_call(finish, out_shape=(jax.ShapeDtypeStruct((ROWS, cols, 128),...  1.6 us

profile of v6, /device:TPU:112, one launch (start us, length us, event | category | flops | bytes accessed | tf_op | source)
XLA Modules:
  0.0 28.0 jit_solution(4378489061356122114)
XLA Ops:
  0.6 0.0 copy-start
  0.6 25.7 %shard_map.68 = (bf16[16,256,128]{2,1,0:T(8,128)(2,1)S(1)}, f32[16,256]{1,0:T(8,128)S(1)}) custom-call(f32[8,2,16,2048]{3,2,1,0:T(8,128)} %x_hbm.1, s32[8,16,2048]{2,1,0:T(8,128)} %e_hbm.1, s32[16,256]{1,0:T(8,128)} %labels_hbm.1, s32[32,128]{1,0:T(8,128)} %bitcast.1, bf16[128,128]{1,0:T(8,128)(2,1)} %constant.2.clone.basis_hbm.basis_ref), custom_call_target="tpu_custom_call" | custom-call | tf_op jit(solution)/shard_map/pallas_call | solution.py:449
  26.4 0.0 copy-done
  26.4 1.6 %shard_map.69 = (bf16[16,256,128]{2,1,0:T(8,128)(2,1)}, f32[16,128]{1,0:T(8,128)}) custom-call(bf16[16,256,128]{2,1,0:T(8,128)(2,1)S(1)} %get-tuple-element.4.coeffs_ref, f32[16,256]{1,0:T(8,128)S(1)} %get-tuple-element.5.total_ref, bf16[128,128]{1,0:T(8,128)(2,1)S(1)} %copy-done), custom_call_target="tpu_custom_call" | custom-call | tf_op jit(solution)/shard_map/pallas_call | solution.py:495
Async XLA Ops:
  0.6 25.8 %copy-start = (bf16[128,128]{1,0:T(8,128)(2,1)S(1)}, bf16[128,128]{1,0:T(8,128)(2,1)}, u32[]{:S(2)}) copy-start(bf16[128,128]{1,0:T(8,128)(2,1)} %constant.2.clone.basis_hbm.basis_ref) | copy-start | bytes 98308

commit v7 on v6

--- a/solution.py
+++ b/solution.py
@@ -17,6 +17,7 @@
 TALL = ROWS + 6
 GROUP = 4
 FAR_FIRST = (4, 3, 5, 2, 6, 1, 7)
+GROUPS = ((3, 4, 5), (6, 7, 8, 9), (10, 11, 12), (13, 14, 15), (2, 1, 0))
 LOG10E = 0.4342944819032518
 STEPS = 65535.0
 MIDDLE = 32768.0
@@ -129,14 +130,20 @@
     def _():
         xin[ROWS + 3 : ROWS + 6] = jnp.zeros((3, 2, 8, wide), F32)
 
-    def send(r):
+    def send(n, rows):
+        here = pl.ds(min(rows), len(rows))
         for k in FAR_FIRST:
             peer = lax.rem(date + k, ndate)
             pltpu.make_async_remote_copy(
-                src_ref=sendbuf.at[r, peer], dst_ref=got.at[r, date],
-                send_sem=send_sem, recv_sem=recv_sem.at[r],
+                src_ref=sendbuf.at[here, peer], dst_ref=got.at[here, date],
+                send_sem=send_sem, recv_sem=recv_sem.at[n],
                 device_id={"date": peer}, device_id_type=MESH).start()
-        pltpu.make_async_copy(sendbuf.at[r, date], got.at[r, date], own_sem.at[r]).start()
+        pltpu.make_async_copy(sendbuf.at[here, date], got.at[here, date], own_sem.at[n]).start()
+
+    def arrive(n, rows):
+        here = pl.ds(min(rows), len(rows))
+        pltpu.make_async_copy(got.at[here, 0 : ndate - 1], got.at[here, 0 : ndate - 1], recv_sem.at[n]).wait()
+        pltpu.make_async_copy(sendbuf.at[here, date], got.at[here, date], own_sem.at[n]).wait()
 
     lanes = lax.broadcasted_iota(jnp.int32, (16, 128), 1)
     width = wide // ndate
@@ -289,7 +296,8 @@
 
         lax.fori_loop(0, 8, lambda t, c: tile(4 * t + 3, tile(4 * t + 2, tile(4 * t + 1, tile(4 * t, c)))), 0)
 
-    def group(rows, init=False):
+    def group(number, init=False):
+        rows = GROUPS[number]
         for n, r in enumerate(rows):
             for h in range(2):
                 tiles = [ein[r, :, b * width + h * 128 : b * width + (h + 1) * 128] for b in range(ndate) for p in range(2)]
@@ -308,7 +316,7 @@
                 filtered = mean + excess * inv * (x - mean)
                 level = (jnp.log(filtered) * LOG10E).astype(BF16).T
                 sendbuf[r, :, :, half_row] = level.reshape(ndate, 16, 128)
-            send(r)
+        send(number, rows)
 
     def spread_step(waits):
         def body(i, carry):
@@ -322,10 +330,10 @@
 
         return body
 
-    def take(rows):
-        for r in rows:
-            pltpu.make_async_copy(got.at[r, 0 : ndate - 1], got.at[r, 0 : ndate - 1], recv_sem.at[r]).wait()
-            pltpu.make_async_copy(sendbuf.at[r, date], got.at[r, date], own_sem.at[r]).wait()
+    def take(numbers):
+        for n in numbers:
+            arrive(n, GROUPS[n])
+        rows = [r for n in numbers for r in GROUPS[n]]
         total = acc[:, :128]
         for r in rows:
             series = got[r].reshape(ndate * 16, width)
@@ -335,11 +343,11 @@
     lax.fori_loop(3, 12, spread_step(True), 0, unroll=True)
     pl.semaphore_wait(barrier, degree)
     halo_out()
-    group([3, 4, 5], init=True)
+    group(0, init=True)
     lax.fori_loop(12, 16, spread_step(True), 0, unroll=True)
-    group([6, 7, 8, 9])
+    group(1)
     lax.fori_loop(16, ROWS + 3, spread_step(True), 0, unroll=True)
-    group([10, 11, 12])
+    group(2)
 
     @pl.when(space < nspace - 1)
     def _():
@@ -347,7 +355,7 @@
         unpack(1, ROWS + 3)
 
     lax.fori_loop(ROWS + 3, ROWS + 6, spread_step(False), 0, unroll=True)
-    group([13, 14, 15])
+    group(3)
 
     @pl.when(space > 0)
     def _():
@@ -355,7 +363,7 @@
         unpack(0, 0)
 
     lax.fori_loop(0, 3, spread_step(False), 0, unroll=True)
-    group([2, 1, 0])
+    group(4)
 
     for copy in small:
         copy.wait()
@@ -381,8 +389,8 @@
     acc[:, :128] = jnp.zeros((4 * ROWS, 128), F32)
     acc[:, 128:] = jnp.broadcast_to(jnp.sum(present, axis=1, keepdims=True), (4 * ROWS, 128))
 
-    take(range(3, ROWS))
-    take(range(3))
+    take(range(4))
+    take([4])
 
     high = date // half
     low = lax.rem(space, 2)

time: 28.6 us -> 28.4 us (level)
  the two profiles are of different devices: /device:TPU:112 before, /device:TPU:1 now
where the time goes in v7:
time: 28.4 us; the launch traced here: 28.3 us
  Pallas kernels  27.6 us (97%)
  between operations  0.65 us (2%)
    pallas_call x1, Pallas kernels, local(): pl.pallas_call(functools.partial(kernel, ndate, nspace, wide), out_shape=...  26 us
    pallas_call x1, Pallas kernels, local(): pl.pallas_call(finish, out_shape=(jax.ShapeDtypeStruct((ROWS, cols, 128),...  1.6 us

profile of v7, /device:TPU:1, one launch (start us, length us, event | category | flops | bytes accessed | tf_op | source)
XLA Modules:
  0.0 28.3 jit_solution(7727791833769344375)
XLA Ops:
  0.6 0.0 copy-start
  0.6 26.0 %shard_map.68 = (bf16[16,256,128]{2,1,0:T(8,128)(2,1)S(1)}, f32[16,256]{1,0:T(8,128)S(1)}) custom-call(f32[8,2,16,2048]{3,2,1,0:T(8,128)} %x_hbm.1, s32[8,16,2048]{2,1,0:T(8,128)} %e_hbm.1, s32[16,256]{1,0:T(8,128)} %labels_hbm.1, s32[32,128]{1,0:T(8,128)} %bitcast.1, bf16[128,128]{1,0:T(8,128)(2,1)} %constant.2.clone.basis_hbm.basis_ref), custom_call_target="tpu_custom_call" | custom-call | tf_op jit(solution)/shard_map/pallas_call | solution.py:457
  26.7 0.0 copy-done
  26.7 1.6 %shard_map.69 = (bf16[16,256,128]{2,1,0:T(8,128)(2,1)}, f32[16,128]{1,0:T(8,128)}) custom-call(bf16[16,256,128]{2,1,0:T(8,128)(2,1)S(1)} %get-tuple-element.4.coeffs_ref, f32[16,256]{1,0:T(8,128)S(1)} %get-tuple-element.5.total_ref, bf16[128,128]{1,0:T(8,128)(2,1)S(1)} %copy-done), custom_call_target="tpu_custom_call" | custom-call | tf_op jit(solution)/shard_map/pallas_call | solution.py:503
Async XLA Ops:
  0.6 26.0 %copy-start = (bf16[128,128]{1,0:T(8,128)(2,1)S(1)}, bf16[128,128]{1,0:T(8,128)(2,1)}, u32[]{:S(2)}) copy-start(bf16[128,128]{1,0:T(8,128)(2,1)} %constant.2.clone.basis_hbm.basis_ref) | copy-start | bytes 98308
